TPU v7x, 32 devices: a whole 2x2x4 slice. The times are simulated.
32 devices in a mesh: lat: 16 (over z, y, x), fld: 2 (over core).
Axes of the slice: x: 2, y: 2, z: 4, core: 2. Of those that a mesh axis runs over, the one named last changes fastest.
Arguments:
- grid_fields: bfloat16 [3, 16, 32, 2, 256], P(None, 'fld', 'lat'), may hold values from -6 to 6
- legendre_basis: bfloat16 [640, 2, 32, 640], P('lat', 'fld'), may hold values from -0.75 to 0.75
- owner_list: int32 [640], replicated, may hold values from 0 to 639, as said below
- wave_speed: float32 [16], P('fld'), may hold values from 1e-06 to 0.01
Outputs:
- balanced_spectra: bfloat16 [640, 2, 3, 16, 640], P('lat', None, None, 'fld')
- balanced_grid: bfloat16 [3, 16, 32, 2, 256], P(None, 'fld', 'lat')
Inputs may be any that keep to these rules, and one draw needn't show every extreme that they name: owner_list is a permutation of the 640 wavenumbers; slot d * 40 + r holds a wavenumber of r * 16 to r * 16 + 15, and for each index d of lat the slots of rounds 2 i and 2 i + 1 hold wavenumbers that add up to (4 i + 2) * 16 - 1.
All inputs are finite; a program needn't handle non-finite values.
Results may differ from a plain program's by a relative error of at most 0.0074.
Values may be sent and summed in bfloat16 or wider, within the bound.
A program may use at most 128 MiB of HBM per device.

v0:
```python
import math

import jax
import jax.numpy as jnp
from jax import lax
from jax.sharding import PartitionSpec as P


def slot_table(pair_index, waves, padded, wave_count):
    points = 20 + 4 * pair_index
    highest = jnp.minimum(wave_count - 1, (points - 1) // 2)
    column = jnp.arange(padded, dtype=jnp.int32)
    phase_steps = column[:, None] * waves[None, :] % points
    angles = phase_steps.astype(jnp.float32) * (
        jnp.float32(2.0 * math.pi) / points.astype(jnp.float32)
    )
    scaling = 1.0 / jnp.sqrt(points.astype(jnp.float32))
    inside = (column[:, None] < points) & (waves[None, :] <= highest)
    cosine = jnp.where(inside, jnp.cos(angles) * scaling, 0.0)
    sine_part = jnp.where(inside, -jnp.sin(angles) * scaling, 0.0)
    stacked = jnp.stack([cosine, sine_part], axis=2).astype(jnp.bfloat16)
    return stacked.reshape(padded, wave_count * 2)


def balance(spectra, speeds, waves):
    totals = jnp.arange(spectra.shape[-1], dtype=jnp.int32)
    degree = totals.astype(jnp.float32)
    laplace = degree * (degree + 1.0)
    stiffness = laplace[None, :] * speeds[:, None]
    retained = 1.0 / (1.0 + stiffness)
    root_term = jnp.sqrt(stiffness)
    removed = stiffness * retained
    vorticity = spectra[:, :, 0]
    divergence = spectra[:, :, 1]
    geopotential = spectra[:, :, 2]
    rossby_part = (root_term * vorticity - geopotential) * retained
    result = jnp.stack(
        [
            retained * vorticity + removed * root_term * rossby_part,
            retained * divergence,
            retained * geopotential - removed * rossby_part,
        ],
        axis=2,
    )
    triangle = totals[None, :] >= waves[:, None]
    return jnp.where(triangle[:, None, None, None, :], result, 0.0)


def per_device(grid_fields, legendre_basis, owner_list, wave_speed):
    position = lax.axis_index("lat")
    slot_count = legendre_basis.shape[0]
    field_count, mode_count, pair_count, hemis, padded = grid_fields.shape
    wave_count = owner_list.shape[0]
    inner = field_count * mode_count * hemis
    own_wave = lax.dynamic_slice_in_dim(owner_list, position * slot_count, slot_count)
    pair_ids = position * pair_count + jnp.arange(pair_count, dtype=jnp.int32)

    def build_table(pair_index):
        return slot_table(pair_index, owner_list, padded, wave_count)

    row_tables = lax.map(build_table, pair_ids)
    grid_rows = jnp.transpose(grid_fields, (2, 0, 1, 3, 4)).reshape(pair_count, inner, padded)
    fourier = jnp.einsum(
        "pjs,pxj->psx", row_tables, grid_rows, preferred_element_type=jnp.float32
    ).astype(jnp.bfloat16)
    flat_rows = fourier.reshape(pair_count, wave_count * 2 * inner)
    columns = lax.all_to_all(flat_rows, "lat", split_axis=1, concat_axis=0, tiled=True)
    half_count = columns.shape[0]
    ordered = jnp.transpose(
        columns.reshape(half_count, slot_count, 2, field_count, mode_count, hemis),
        (1, 2, 3, 4, 5, 0),
    )
    full_basis = lax.all_gather(legendre_basis, "fld", axis=1, tiled=True)
    spectra = jnp.einsum(
        "stfkhp,shpn->stfkn", ordered, full_basis, preferred_element_type=jnp.float32
    )
    balanced = balance(spectra, wave_speed, own_wave).astype(jnp.bfloat16)
    returned = jnp.einsum(
        "stfkn,shpn->stfkhp", balanced, full_basis, preferred_element_type=jnp.float32
    ).astype(jnp.bfloat16)
    outgoing = jnp.transpose(returned, (5, 0, 1, 2, 3, 4)).reshape(
        half_count, slot_count * 2 * inner
    )
    back_rows = lax.all_to_all(outgoing, "lat", split_axis=0, concat_axis=1, tiled=True)
    weights = jnp.where(owner_list == 0, 1.0, 2.0).astype(jnp.bfloat16)
    scaled = (
        back_rows.reshape(pair_count, wave_count, 2 * inner) * weights[None, :, None]
    ).reshape(pair_count, wave_count * 2, inner)
    grid_new = jnp.einsum(
        "psx,pjs->pxj", scaled, row_tables, preferred_element_type=jnp.float32
    ).astype(jnp.bfloat16)
    balanced_grid = jnp.transpose(
        grid_new.reshape(pair_count, field_count, mode_count, hemis, padded), (1, 2, 0, 3, 4)
    )
    return (balanced, balanced_grid)


def solution(mesh):
    placed = (P(None, "fld", "lat", None, None), P("lat", "fld", None, None), P(), P("fld"))
    return jax.shard_map(
        per_device,
        mesh=mesh,
        in_specs=placed,
        out_specs=(P("lat", None, None, "fld", None), P(None, "fld", "lat", None, None)),
        check_vma=False,
    )
```

profile of v0, /device:TPU:0, one launch (start us, length us, event | category | flops | bytes accessed | tf_op | source)
XLA Modules:
  0.0 319.8 jit_solution(8960347931420876565)
XLA Ops:
  7.2 0.7 all-gather.2.cloned.1.call-update
  8.0 153.7 %while.15 = (s32[]{:T(128)}, bf16[2,256,1280]{1,2,0:T(8,128)(2,1)S(1)}, s32[2]{0:T(128)S(1)}, s32[640]{0:T(1024)S(1)}, s32[]{:T(128)}, /*index=5*/s32[1]{0:T(128...) while((s32[]{:T(128)}, bf16[2,256,1280]{1,2,0:T(8,128)(2,1)S(1)}, ...), condition=%wide.region_1.2_spmd, body=%wide.region_0.1_spmd.sunk | while | flops 4260762 | bytes 4594843 | solution.py:61
  8.0 0.6 dynamic_slice.16
  9.4 73.7 %fusion.30 = (bf16[256,640,1]{0,2,1:T(2,128)(2,1)S(1)}, bf16[256,640,1]{0,2,1:T(2,128)(2,1)S(1)}) fusion(pred[640]{0:T(1024)(128)(4,1)S(1)} %broadcast_compare_fusion.2, pred[256]{0:T(512)(128)(4,1)S(1)} %iota_compare_fusion.3, f32[]{:T(128)S(6)} %sqrt.18, f32[]{:T(128)S(6)} %div.45, pred[]{:T(512)S(6)} %lt.87, s32[]{:T(128)S(6)} %select_n.125, ...), kind=kLoop, calls=%fused_computation.5.clone.1 | loop fusion | flops 2949120 | bytes 658829 | tf_op jit(solution)/shard_map/convert
  83.1 1.5 pad_maximum_fusion.2
  86.3 73.7 %fusion.30 = (bf16[256,640,1]{0,2,1:T(2,128)(2,1)S(1)}, bf16[256,640,1]{0,2,1:T(2,128)(2,1)S(1)}) fusion(pred[640]{0:T(1024)(128)(4,1)S(1)} %broadcast_compare_fusion.2, pred[256]{0:T(512)(128)(4,1)S(1)} %iota_compare_fusion.3, f32[]{:T(128)S(6)} %sqrt.18, f32[]{:T(128)S(6)} %div.45, pred[]{:T(512)S(6)} %lt.87, s32[]{:T(128)S(6)} %select_n.125, ...), kind=kLoop, calls=%fused_computation.5.clone.1 | loop fusion | flops 2949120 | bytes 658829 | tf_op jit(solution)/shard_map/convert
  160.0 1.5 pad_maximum_fusion.2
  162.6 0.6 all_to_all.24
  163.3 0.9 copy.22
  164.1 8.3 %all-to-all-start = ((bf16[2,16,3840]{2,0,1:T(2,128)(2,1)}), bf16[2,16,3840]{2,0,1:T(2,128)(2,1)S(1)}, u32[]{:S(2)}, u32[]{:S(2)}) async-start(bf16[2,16,3840]{2,0,1:T(2,128)(2,1)} %copy.22), calls=%async_computation | async-start | bytes 491520 | tf_op jit(solution)/shard_map/all_to_all | solution.py:67
  172.7 9.3 %all-to-all-done = bf16[2,16,3840]{2,0,1:T(2,128)(2,1)S(1)} async-done(((bf16[2,16,3840]{2,0,1:T(2,128)(2,1)}), bf16[2,16,3840]{2,0,1:T(2,128)(2,1)S(1)}, u32[]{:S(2)}, u32[]{:S(2)}) %all-to-all-start) | async-done | bytes 245792 | tf_op jit(solution)/shard_map/all_to_all | solution.py:67
  182.0 35.2 %reshape.375 = bf16[32,40,2,3,8,2]{5,4,3,2,1,0:T(8,128)(2,1)} reshape(bf16[16,2,3840]{2,1,0:T(2,128)(2,1)S(1)} %bitcast.49) | data formatting | bytes 491520 | tf_op jit(solution)/shard_map/reshape | solution.py:70
  217.2 17.6 %copy.23 = bf16[32,40,2,3,8,2]{0,4,5,3,2,1:T(8,128)(2,1)S(1)} copy(bf16[32,40,2,3,8,2]{5,4,3,2,1,0:T(8,128)(2,1)} %reshape.375) | data formatting | bytes 491520 | tf_op jit(solution)/shard_map/reshape | solution.py:70
  234.8 2.8 fusion.8
  237.6 0.7 multiply_add_fusion
  238.3 1.0 fusion.2
  239.3 1.0 copy-done
  240.3 3.2 fusion.16
  243.5 26.3 %copy.24 = bf16[32,40,2,3,8,2]{5,4,3,2,1,0:T(8,128)(2,1)} copy(bf16[32,40,2,3,8,2]{0,4,5,3,2,1:T(8,128)(2,1)S(1)} %fusion.16) | data formatting | bytes 491520 | tf_op jit(solution)/shard_map/convert_element_type | solution.py:80
  269.7 28.4 %all_to_all.27 = bf16[16,2,3840]{2,1,0:T(2,128)(2,1)} reshape(bf16[32,40,2,3,8,2]{5,4,3,2,1,0:T(8,128)(2,1)} %copy.24) | data formatting | bytes 491520 | tf_op jit(solution)/shard_map/all_to_all | solution.py:84
  298.1 3.7 %all-to-all-start.1 = ((bf16[16,2,3840]{2,1,0:T(2,128)(2,1)}), bf16[16,2,3840]{2,1,0:T(2,128)(2,1)S(1)}, u32[]{:S(2)}, u32[]{:S(2)}) async-start(bf16[16,2,3840]{2,1,0:T(2,128)(2,1)} %all_to_all.27), calls=%async_computation.1 | async-start | bytes 491520 | tf_op jit(solution)/shard_map/all_to_all | solution.py:84
  302.2 8.5 %all-to-all-done.1 = bf16[16,2,3840]{2,1,0:T(2,128)(2,1)S(1)} async-done(((bf16[16,2,3840]{2,1,0:T(2,128)(2,1)}), bf16[16,2,3840]{2,1,0:T(2,128)(2,1)S(1)}, u32[]{:S(2)}, u32[]{:S(2)}) %all-to-all-start.1) | async-done | bytes 245792 | tf_op jit(solution)/shard_map/all_to_all | solution.py:84
  310.8 0.9 reshape.376
  312.3 0.7 copy.38
  (39 shorter events, 3.4 us)
Async XLA Ops:
  7.2 0.8 copy-start.5
  7.2 0.8 copy-start.4
  7.2 227.6 %all-gather.2.cloned.1.call-start = ((), (), s32[]{:S(2)}) async-start(), calls=%async_computation.2 | async-start | bytes 4915200 | tf_op jit(solution)/shard_map/all_gather | solution.py:73
  161.8 1.5 copy-start.2
  162.3 10.4 %copy-start.6 = (f32[8]{0:T(128)S(1)}, f32[8]{0:T(128)}, u32[]{:S(2)}) copy-start(f32[8]{0:T(128)} %param.9) | copy-start | bytes 100
  164.1 17.9 %all-to-all-start = ((bf16[2,16,3840]{2,0,1:T(2,128)(2,1)}), bf16[2,16,3840]{2,0,1:T(2,128)(2,1)S(1)}, u32[]{:S(2)}, u32[]{:S(2)}) async-start(bf16[2,16,3840]{2,0,1:T(2,128)(2,1)} %copy.22), calls=%async_computation | async-start | bytes 491520 | tf_op jit(solution)/shard_map/all_to_all | solution.py:67
  238.3 1.9 copy-start
  240.2 3.2 %copy-start.1 = (bf16[40,2,3,8,640]{4,3,2,1,0:T(8,128)(2,1)}, bf16[40,2,3,8,640]{4,3,2,1,0:T(8,128)(2,1)S(1)}, u32[]{:S(2)}) copy-start(bf16[40,2,3,8,640]{4,3,2,1,0:T(8,128)(2,1)S(1)} %fusion.2) | copy-start | bytes 7372804
  298.1 13.6 %copy-start.3 = (bf16[2,256,1280]{1,2,0:T(8,128)(2,1)S(1)}, bf16[2,256,1280]{1,2,0:T(8,128)(2,1)}, u32[]{:S(2)}) copy-start(bf16[2,256,1280]{1,2,0:T(8,128)(2,1)} %copy-done.2) | copy-start | bytes 3932164
  298.1 12.6 %all-to-all-start.1 = ((bf16[16,2,3840]{2,1,0:T(2,128)(2,1)}), bf16[16,2,3840]{2,1,0:T(2,128)(2,1)S(1)}, u32[]{:S(2)}, u32[]{:S(2)}) async-start(bf16[16,2,3840]{2,1,0:T(2,128)(2,1)} %all_to_all.27), calls=%async_computation.1 | async-start | bytes 491520 | tf_op jit(solution)/shard_map/all_to_all | solution.py:84
Sparse Core Ops, SparseCore 0:
  9.6 15.0 all-gather.1
where the time goes:
time: 320 us
  other arithmetic  152 us (48%)
  local copies, waits for them, and re-layouts  114 us (36%)
  waiting for transfers between devices  18.5 us (6%)
  between operations  14.3 us (4%)
  starting transfers between devices  12 us (4%)
  matrix products  7.04 us (2%)
    another operation x2, other arithmetic  147 us
    reshape x2, local copies, waits for them, and re-layouts, per_device(): columns.reshape(half_count, slot_count, 2, field_count, mode_count, hemis)  52.8 us
    all_to_all x2, local copies, waits for them, and re-layouts, per_device(): lax.all_to_all(outgoing, 'lat', split_axis=0, concat_axis=1, tiled=True)  28.4 us
    convert_element_type x1, local copies, waits for them, and re-layouts, per_device(): returned = jnp.einsum('stfkn,shpn->stfkhp', balanced, full_basis, preferr...  26.3 us
    all_to_all x1, waiting for transfers between devices, per_device(): lax.all_to_all(flat_rows, 'lat', split_axis=1, concat_axis=0, tiled=True)  9.27 us
    all_to_all x1, waiting for transfers between devices, per_device(): lax.all_to_all(outgoing, 'lat', split_axis=0, concat_axis=1, tiled=True)  8.54 us
    all_to_all x1, starting transfers between devices, per_device(): lax.all_to_all(flat_rows, 'lat', split_axis=1, concat_axis=0, tiled=True)  8.32 us
  transfers between devices with their start and end apart: 3, of which 2 were waited for; matrix products, arithmetic and copies ran while one was open for 65% of the time, Pallas kernels for 0%

commit v1 on v0

v1 whole, which is shorter than its diff:
```python
import functools

import jax
import jax.numpy as jnp
from jax import lax
from jax.experimental import pallas as pl
from jax.experimental.pallas import tpu as pltpu
from jax.sharding import PartitionSpec as P

MESH = pl.DeviceIdType.MESH

COS_SERIES = (
    1.0,
    -19.73920440673828,
    64.93911743164062,
    -85.45014190673828,
    60.16762924194336,
    -25.967599868774414,
    6.528658390045166,
)
SIN_SERIES = (
    6.2831854820251465,
    -41.34170150756836,
    81.60513305664062,
    -76.70301818847656,
    42.02592849731445,
    -14.899847030639648,
    3.2381374835968018,
)


def polynomial(series, argument):
    total = jnp.full_like(argument, series[-1])
    for coefficient in series[-2::-1]:
        total = total * argument + coefficient
    return total


def round_up(value, multiple):
    return -(-value // multiple) * multiple


def kernel(
    sizes,
    rows_ref,
    basis_ref,
    owner_ref,
    speed_ref,
    spectra_ref,
    grid_ref,
    table,
    basis,
    forward_out,
    forward_in,
    backward_out,
    backward_in,
    by_round,
    own_sem,
    basis_sems,
    forward_sems,
    backward_sems,
):
    (ranks, halves, slots, rounds, padded_rounds, fields, modes, pairs, wave_count) = sizes
    inner = fields * modes
    half_count = ranks * pairs
    columns = table.shape[2] // 2
    block_rows = pairs * padded_rounds
    totals = basis.shape[3]
    me = lax.axis_index("lat")
    hemisphere = lax.axis_index("fld")
    other = halves - 1 - hemisphere

    own_copy = pltpu.make_async_copy(
        basis_ref.at[pl.ds(0, rounds), 0], basis.at[hemisphere], own_sem
    )
    own_copy.start()

    barrier = pltpu.get_barrier_semaphore()

    def greet(step, carry):
        peer = lax.rem(me + step, ranks)
        pl.semaphore_signal(
            barrier, inc=1, device_id=(peer, hemisphere), device_id_type=MESH
        )
        return carry

    lax.fori_loop(1, ranks, greet, 0)
    pl.semaphore_signal(barrier, inc=1, device_id=(me, other), device_id_type=MESH)

    together = max(1, 16 // padded_rounds)
    chunk = together * padded_rounds
    row_index = lax.broadcasted_iota(jnp.int32, (chunk, columns), 0)
    column = lax.broadcasted_iota(jnp.int32, (chunk, columns), 1)
    column_f = column.astype(jnp.float32)

    def fill(step, carry):
        wave = jnp.full((chunk, columns), -1, jnp.int32)
        for part in range(together):
            for index in range(rounds):
                number = owner_ref[(step * together + part) * slots + index]
                wave = jnp.where(row_index == part * padded_rounds + index, number, wave)
        product = wave.astype(jnp.float32) * column_f
        for pair in range(pairs):
            points = 20 + 4 * (me * pairs + pair)
            highest = jnp.minimum(wave_count - 1, (points - 1) // 2)
            points_f = jnp.full((1, columns), points, jnp.int32).astype(jnp.float32)
            inverse = 1.0 / points_f
            scaling = lax.rsqrt(points_f)
            turns = jnp.floor(product * inverse + 0.5)
            angle = (product - turns * points_f) * inverse
            square = angle * angle
            inside = (column < points) & (wave <= highest) & (wave >= 0)
            scale = jnp.where(inside, scaling, 0.0)
            cosine = polynomial(COS_SERIES, square) * scale
            sine = polynomial(SIN_SERIES, square) * (angle * scale)
            where = pl.ds(pl.multiple_of(step * chunk, chunk), chunk)
            table[pair, where, 0:columns] = cosine.astype(jnp.bfloat16)
            table[pair, where, columns : 2 * columns] = (-sine).astype(jnp.bfloat16)
        return carry

    lax.fori_loop(0, ranks // together, fill, 0, unroll=2)

    blocks = []
    width = halves * inner
    for pair in range(pairs):
        values = rows_ref[pair * width : (pair + 1) * width, 0:columns]
        empty = jnp.zeros_like(values)
        both = jnp.concatenate(
            [
                jnp.concatenate([values, empty], axis=1),
                jnp.concatenate([empty, values], axis=1),
            ],
            axis=0,
        )
        found = lax.dot_general(
            table[pair], both, (((1,), (1,)), ((), ())), preferred_element_type=jnp.float32
        )
        blocks.append(found.reshape(ranks, padded_rounds, 2 * width))
    forward_out[:, :, 0 : 2 * width] = jnp.concatenate(blocks, axis=1).astype(jnp.bfloat16)

    pl.semaphore_wait(barrier, ranks)

    def send(out, into, sems):
        def one(step, carry):
            peer = lax.rem(me + step, ranks)
            pltpu.make_async_remote_copy(
                src_ref=out.at[peer],
                dst_ref=into.at[me],
                send_sem=sems.at[0],
                recv_sem=sems.at[1],
                device_id=(peer, hemisphere),
                device_id_type=MESH,
            ).start()
            return carry

        lax.fori_loop(1, ranks, one, 0)
        into[me] = out[me]

    def wait(ref, sem):
        part = ref.at[pl.ds(0, ranks - 1)]
        pltpu.make_async_copy(part, part, sem).wait()

    send(forward_out, forward_in, forward_sems)
    basis_copy = pltpu.make_async_remote_copy(
        src_ref=basis_ref.at[pl.ds(0, rounds), 0],
        dst_ref=basis.at[hemisphere],
        send_sem=basis_sems.at[0],
        recv_sem=basis_sems.at[1],
        device_id=(me, other),
        device_id_type=MESH,
    )
    basis_copy.start()

    mode_index = lax.broadcasted_iota(jnp.int32, (modes, totals), 0)
    degree_i = lax.broadcasted_iota(jnp.int32, (modes, totals), 1)
    degree = degree_i.astype(jnp.float32)
    speeds = jnp.zeros((modes, totals), jnp.float32)
    for mode in range(modes):
        speeds = jnp.where(mode_index == mode, speed_ref[mode], speeds)
    stiffness = degree * (degree + 1.0) * speeds
    retained = 1.0 / (1.0 + stiffness)
    root_term = jnp.sqrt(stiffness)
    removed = stiffness * retained

    wait(forward_in, forward_sems.at[1])
    by_round[...] = forward_in[...].astype(jnp.float32).reshape(by_round.shape)
    own_copy.wait()
    basis_copy.wait_recv()

    incoming = [
        by_round[pl.ds(index, half_count, stride=padded_rounds), :] for index in range(rounds)
    ]
    by_round[...] = jnp.zeros_like(by_round)

    for index in range(rounds):
        number = owner_ref[me * slots + index]
        turned = incoming[index].T
        spectra = jnp.zeros((2 * inner, totals), jnp.float32)
        for side in range(halves):
            coefficients = jnp.concatenate(
                [
                    turned[part * width + side * inner : part * width + (side + 1) * inner]
                    for part in range(2)
                ],
                axis=0,
            ).astype(jnp.bfloat16)
            spectra = spectra + jnp.dot(
                coefficients, basis[side, index], preferred_element_type=jnp.float32
            )
        kept = degree_i >= number
        pieces = []
        for part in range(2):
            first = part * inner
            vorticity = spectra[first : first + modes]
            divergence = spectra[first + modes : first + 2 * modes]
            geopotential = spectra[first + 2 * modes : first + 3 * modes]
            rossby_part = (root_term * vorticity - geopotential) * retained
            for value in (
                retained * vorticity + removed * root_term * rossby_part,
                retained * divergence,
                retained * geopotential - removed * rossby_part,
            ):
                pieces.append(jnp.where(kept, value, 0.0))
        balanced = jnp.concatenate(pieces, axis=0).astype(jnp.bfloat16)
        spectra_ref[index] = balanced
        weight = jnp.where(number == 0, 1.0, 2.0)
        sides = [
            lax.dot_general(
                balanced,
                basis[side, index],
                (((1,), (1,)), ((), ())),
                preferred_element_type=jnp.float32,
            )
            for side in range(halves)
        ]
        ordered = [
            sides[side][part * inner : (part + 1) * inner]
            for part in range(2)
            for side in range(halves)
        ]
        spare = by_round.shape[1] - 2 * width
        if spare:
            ordered.append(jnp.zeros((spare, half_count), jnp.float32))
        by_round[pl.ds(index, half_count, stride=padded_rounds), :] = (
            jnp.concatenate(ordered, axis=0).T * weight
        )

    backward_out[...] = by_round[...].astype(jnp.bfloat16).reshape(backward_out.shape)
    send(backward_out, backward_in, backward_sems)
    wait(backward_in, backward_sems.at[1])

    for pair in range(pairs):
        first = pair * padded_rounds
        arrived = (
            backward_in[...]
            .astype(jnp.float32)[:, first : first + padded_rounds]
            .reshape(ranks * padded_rounds, by_round.shape[1])
            .T
        )
        result = jnp.zeros((width, columns), jnp.float32)
        for part in range(2):
            result = result + jnp.dot(
                arrived[part * width : (part + 1) * width].astype(jnp.bfloat16),
                table[pair, :, part * columns : (part + 1) * columns],
                preferred_element_type=jnp.float32,
            )
        grid_ref[pair * width : (pair + 1) * width, 0:columns] = result.astype(jnp.bfloat16)
        if columns < grid_ref.shape[1]:
            grid_ref[pair * width : (pair + 1) * width, columns:] = jnp.zeros(
                (width, grid_ref.shape[1] - columns), jnp.bfloat16
            )

    basis_copy.wait_send()
    wait(forward_out, forward_sems.at[0])
    wait(backward_out, backward_sems.at[0])


def per_device(ranks, halves, grid_fields, legendre_basis, owner_list, wave_speed):
    fields, modes, pairs, hemis, padded = grid_fields.shape
    slots, _, half_count, totals = legendre_basis.shape
    wave_count = owner_list.shape[0]
    longest = 20 + 4 * (half_count - 1)
    highest = min(wave_count - 1, (longest - 1) // 2)
    rounds = min(slots, highest // ranks + 1)
    padded_rounds = round_up(rounds, 8)
    columns = min(padded, round_up(longest, 128))
    lanes = round_up(2 * hemis * fields * modes, 128)
    block_rows = pairs * padded_rounds
    sizes = (ranks, halves, slots, rounds, padded_rounds, fields, modes, pairs, wave_count)
    grid_rows = jnp.transpose(grid_fields, (2, 3, 0, 1, 4)).reshape(-1, padded)
    block = pltpu.VMEM((ranks, block_rows, lanes), jnp.bfloat16)
    spectra, rows = pl.pallas_call(
        functools.partial(kernel, sizes),
        out_shape=(
            jax.ShapeDtypeStruct((rounds, 2 * fields * modes, totals), jnp.bfloat16),
            jax.ShapeDtypeStruct(grid_rows.shape, jnp.bfloat16),
        ),
        in_specs=[
            pl.BlockSpec(memory_space=pltpu.VMEM),
            pl.BlockSpec(memory_space=pltpu.HBM),
            pl.BlockSpec(memory_space=pltpu.SMEM),
            pl.BlockSpec(memory_space=pltpu.SMEM),
        ],
        out_specs=[pl.BlockSpec(memory_space=pltpu.VMEM)] * 2,
        scratch_shapes=[
            pltpu.VMEM((pairs, ranks * padded_rounds, 2 * columns), jnp.bfloat16),
            pltpu.VMEM((hemis, rounds, half_count, totals), jnp.bfloat16),
            block,
            block,
            block,
            block,
            pltpu.VMEM((ranks * block_rows, lanes), jnp.float32),
            pltpu.SemaphoreType.DMA,
            pltpu.SemaphoreType.DMA((2,)),
            pltpu.SemaphoreType.DMA((2,)),
            pltpu.SemaphoreType.DMA((2,)),
        ],
        compiler_params=pltpu.CompilerParams(
            collective_id=0, has_side_effects=True, vmem_limit_bytes=48 * 2**20
        ),
    )(grid_rows, legendre_basis, owner_list, wave_speed)
    balanced = spectra.reshape(rounds, 2, fields, modes, totals)
    if rounds < slots:
        balanced = jnp.pad(balanced, ((0, slots - rounds),) + ((0, 0),) * 4)
    balanced_grid = jnp.transpose(
        rows.reshape(pairs, hemis, fields, modes, padded), (2, 3, 0, 1, 4)
    )
    return (balanced, balanced_grid)


def solution(mesh):
    placed = (P(None, "fld", "lat", None, None), P("lat", "fld", None, None), P(), P("fld"))
    return jax.shard_map(
        functools.partial(per_device, mesh.shape["lat"], mesh.shape["fld"]),
        mesh=mesh,
        in_specs=placed,
        out_specs=(P("lat", None, None, "fld", None), P(None, "fld", "lat", None, None)),
        check_vma=False,
    )
```

time: 320 us -> 25.4 us (0.08)
  other arithmetic: 152 us -> 0 us
  local copies, waits for them, and re-layouts: 114 us -> 5.86 us
  Pallas kernels: 0 us -> 18.7 us
  waiting for transfers between devices: 18.5 us -> 0 us
  between operations: 14.3 us -> 0.64 us
  starting transfers between devices: 12 us -> 0 us
  matrix products: 7.04 us -> 0 us
    another operation x4 -> x0, other arithmetic: 150 us -> none
    reshape x5 -> x1, local copies, waits for them, and re-layouts: 54.4 us -> 0.66 us  [per_device(): rows.reshape(pairs, hemis, fields, modes, padded)]
    all_to_all x4 -> x0, local copies, waits for them, and re-layouts: 29.9 us -> none  [the longest x2 28.4 us: per_device(): lax.all_to_all(outgoing, 'lat', split_axis=0, concat_axis=1, tiled=True)]
    convert_element_type x4 -> x0, local copies, waits for them, and re-layouts: 27.1 us -> none  [the longest x1 26.3 us: per_device(): returned = jnp.einsum('stfkn,shpn->stfkhp', balanced, full_basis, preferr...]
    pallas_call x0 -> x1, Pallas kernels: none -> 18.7 us  [per_device(): pl.pallas_call(functools.partial(kernel, sizes), out_shape=(jax.ShapeDtyp...]
    all_to_all x2 -> x0, waiting for transfers between devices: 17.8 us -> none  [the longest x1 9.27 us: per_device(): lax.all_to_all(flat_rows, 'lat', split_axis=1, concat_axis=0, tiled=True)]
    all_to_all x2 -> x0, starting transfers between devices: 12 us -> none  [the longest x1 8.32 us: per_device(): lax.all_to_all(flat_rows, 'lat', split_axis=1, concat_axis=0, tiled=True)]
    dot_general x4 -> x0, matrix products: 7.04 us -> none  [the longest x1 3.19 us: per_device(): jnp.einsum('stfkn,shpn->stfkhp', balanced, full_basis, preferred_element_...]
  transfers between devices with their start and end apart: 3 -> 0, of which waited for: 2 -> 0; matrix products, arithmetic and copies ran while one was open for 65% -> 0% of each run, Pallas kernels for 0% -> 0%
where the time goes in v1:
time: 25.4 us; the launch traced here: 25.2 us
  Pallas kernels  18.7 us (74%)
  local copies, waits for them, and re-layouts  5.86 us (23%)
  between operations  0.64 us (3%)
    pallas_call x1, Pallas kernels, per_device(): pl.pallas_call(functools.partial(kernel, sizes), out_shape=(jax.ShapeDtyp...  18.7 us
    unnamed x6, local copies, waits for them, and re-layouts  2.77 us
    pad x1, local copies, waits for them, and re-layouts, per_device(): balanced = jnp.pad(balanced, ((0, slots - rounds),) + ((0, 0),) * 4)  1.63 us
    transpose x1, local copies, waits for them, and re-layouts, per_device(): grid_rows = jnp.transpose(grid_fields, (2, 3, 0, 1, 4)).reshape(-1, padded)  0.81 us
    reshape x1, local copies, waits for them, and re-layouts, per_device(): rows.reshape(pairs, hemis, fields, modes, padded)  0.66 us

profile of v1, /device:TPU:0, one launch (start us, length us, event | category | flops | bytes accessed | tf_op | source)
XLA Modules:
  0.0 25.2 jit_solution(3899934446821633445)
XLA Ops:
  0.6 0.8 %copy.6 = bf16[2,2,3,8,256]{4,3,2,1,0:T(8,128)(2,1)S(1)} copy(bf16[2,2,3,8,256]{4,1,0,3,2:T(2,128)(2,1)} %bitcast.10) | data formatting | bytes 98304 | tf_op jit(solution)/shard_map/transpose | solution.py:290
  1.4 0.0 copy-start
  1.4 1.4 %copy-done = bf16[40,1,32,640]{3,2,1,0:T(8,128)(2,1)S(1)} copy-done((bf16[40,1,32,640]{3,2,1,0:T(8,128)(2,1)S(1)}, bf16[40,1,32,640]{3,2,1,0:T(8,128)(2,1)}, u32[]{:S(2)}) %copy-start) | copy-done | bytes 1638424
  2.9 0.0 copy-start.1
  2.9 0.7 %copy-done.1 = s32[640]{0:T(1024)S(1)} copy-done((s32[640]{0:T(1024)S(1)}, s32[640]{0:T(1024)}, u32[]{:S(2)}) %copy-start.1) | copy-done | bytes 2584
  3.6 0.0 copy-start.2
  3.6 0.7 %copy-done.2 = f32[8]{0:T(128)S(1)} copy-done((f32[8]{0:T(128)S(1)}, f32[8]{0:T(128)}, u32[]{:S(2)}) %copy-start.2) | copy-done | bytes 56
  4.2 18.7 %shard_map.59 = (bf16[5,48,640]{2,1,0:T(8,128)(2,1)S(1)}, bf16[96,256]{1,0:T(8,128)(2,1)S(1)}) custom-call(bf16[96,256]{1,0:T(8,128)(2,1)S(1)} %bitcast.8, bf16[40,1,32,640]{3,2,1,0:T(8,128)(2,1)S(1)} %copy-done, s32[640]{0:T(1024)S(1)} %copy-done.1, f32[8]{0:T(128)S(1)} %copy-done.2), custom_call_target="tpu_custom_call" | custom-call | tf_op jit(solution)/shard_map/pallas_call | solution.py:292
  22.9 0.7 %copy.9 = bf16[2,2,3,8,256]{4,1,0,3,2:T(2,128)(2,1)} copy(bf16[2,2,3,8,256]{4,3,2,1,0:T(8,128)(2,1)S(1)} %bitcast.9) | data formatting | bytes 98304 | tf_op jit(solution)/shard_map/reshape | solution.py:326
  23.6 1.6 %pad.4 = bf16[40,2,3,8,640]{4,3,2,1,0:T(8,128)(2,1)} pad(bf16[5,2,3,8,640]{4,3,2,1,0:T(8,128)(2,1)S(1)} %bitcast.7, bf16[]{:T(256)} %constant.2.clone.1), padding=0_35x0_0x0_0x0_0x0_0 | pad | bytes 2764802 | tf_op jit(solution)/shard_map/jit(_pad)/pad | solution.py:324
Async XLA Ops:
  1.4 1.4 %copy-start = (bf16[40,1,32,640]{3,2,1,0:T(8,128)(2,1)S(1)}, bf16[40,1,32,640]{3,2,1,0:T(8,128)(2,1)}, u32[]{:S(2)}) copy-start(bf16[40,1,32,640]{3,2,1,0:T(8,128)(2,1)} %basis_ref.1) | copy-start | bytes 4915204
  2.9 0.7 %copy-start.1 = (s32[640]{0:T(1024)S(1)}, s32[640]{0:T(1024)}, u32[]{:S(2)}) copy-start(s32[640]{0:T(1024)} %owner_ref.1) | copy-start | bytes 7684
  3.6 0.7 %copy-start.2 = (f32[8]{0:T(128)S(1)}, f32[8]{0:T(128)}, u32[]{:S(2)}) copy-start(f32[8]{0:T(128)} %speed_ref.1) | copy-start | bytes 100

commit v2 on v1

--- a/solution.py
+++ b/solution.py
@@ -10,22 +10,20 @@
 MESH = pl.DeviceIdType.MESH
 
 COS_SERIES = (
-    1.0,
-    -19.73920440673828,
-    64.93911743164062,
-    -85.45014190673828,
-    60.16762924194336,
-    -25.967599868774414,
-    6.528658390045166,
+    0.9999992251396179,
+    -19.738981246948242,
+    64.92865753173828,
+    -85.27162170410156,
+    58.79049301147461,
+    -21.07110595703125,
 )
 SIN_SERIES = (
-    6.2831854820251465,
-    -41.34170150756836,
-    81.60513305664062,
-    -76.70301818847656,
-    42.02592849731445,
-    -14.899847030639648,
-    3.2381374835968018,
+    6.283185005187988,
+    -41.341590881347656,
+    81.59994506835938,
+    -76.61447143554688,
+    41.3428840637207,
+    -12.471243858337402,
 )
 
 
@@ -42,11 +40,11 @@
 
 def kernel(
     sizes,
-    rows_ref,
+    rows_hbm,
     basis_ref,
-    owner_ref,
-    speed_ref,
-    spectra_ref,
+    owner_hbm,
+    speed_hbm,
+    spectra_hbm,
     grid_ref,
     table,
     basis,
@@ -55,7 +53,12 @@
     backward_out,
     backward_in,
     by_round,
+    rows_ref,
+    owner_ref,
+    speed_ref,
+    spectra_ref,
     own_sem,
+    local_sems,
     basis_sems,
     forward_sems,
     backward_sems,
@@ -73,6 +76,13 @@
     own_copy = pltpu.make_async_copy(
         basis_ref.at[pl.ds(0, rounds), 0], basis.at[hemisphere], own_sem
     )
+    owner_copy = pltpu.make_async_copy(owner_hbm, owner_ref, local_sems.at[0])
+    speed_copy = pltpu.make_async_copy(speed_hbm, speed_ref, local_sems.at[1])
+    rows_copy = pltpu.make_async_copy(rows_hbm, rows_ref, local_sems.at[2])
+    spectra_copy = pltpu.make_async_copy(spectra_ref, spectra_hbm, local_sems.at[3])
+    owner_copy.start()
+    speed_copy.start()
+    rows_copy.start()
     own_copy.start()
 
     barrier = pltpu.get_barrier_semaphore()
@@ -118,7 +128,9 @@
             table[pair, where, columns : 2 * columns] = (-sine).astype(jnp.bfloat16)
         return carry
 
+    owner_copy.wait()
     lax.fori_loop(0, ranks // together, fill, 0, unroll=2)
+    rows_copy.wait()
 
     blocks = []
     width = halves * inner
@@ -171,6 +183,7 @@
     )
     basis_copy.start()
 
+    speed_copy.wait()
     mode_index = lax.broadcasted_iota(jnp.int32, (modes, totals), 0)
     degree_i = lax.broadcasted_iota(jnp.int32, (modes, totals), 1)
     degree = degree_i.astype(jnp.float32)
@@ -247,6 +260,7 @@
 
     backward_out[...] = by_round[...].astype(jnp.bfloat16).reshape(backward_out.shape)
     send(backward_out, backward_in, backward_sems)
+    spectra_copy.start()
     wait(backward_in, backward_sems.at[1])
 
     for pair in range(pairs):
@@ -270,6 +284,7 @@
                 (width, grid_ref.shape[1] - columns), jnp.bfloat16
             )
 
+    spectra_copy.wait()
     basis_copy.wait_send()
     wait(forward_out, forward_sems.at[0])
     wait(backward_out, backward_sems.at[0])
@@ -295,13 +310,11 @@
             jax.ShapeDtypeStruct((rounds, 2 * fields * modes, totals), jnp.bfloat16),
             jax.ShapeDtypeStruct(grid_rows.shape, jnp.bfloat16),
         ),
-        in_specs=[
+        in_specs=[pl.BlockSpec(memory_space=pltpu.HBM)] * 4,
+        out_specs=[
+            pl.BlockSpec(memory_space=pltpu.HBM),
             pl.BlockSpec(memory_space=pltpu.VMEM),
-            pl.BlockSpec(memory_space=pltpu.HBM),
-            pl.BlockSpec(memory_space=pltpu.SMEM),
-            pl.BlockSpec(memory_space=pltpu.SMEM),
         ],
-        out_specs=[pl.BlockSpec(memory_space=pltpu.VMEM)] * 2,
         scratch_shapes=[
             pltpu.VMEM((pairs, ranks * padded_rounds, 2 * columns), jnp.bfloat16),
             pltpu.VMEM((hemis, rounds, half_count, totals), jnp.bfloat16),
@@ -310,13 +323,18 @@
             block,
             block,
             pltpu.VMEM((ranks * block_rows, lanes), jnp.float32),
+            pltpu.VMEM(grid_rows.shape, jnp.bfloat16),
+            pltpu.SMEM(owner_list.shape, jnp.int32),
+            pltpu.SMEM(wave_speed.shape, jnp.float32),
+            pltpu.VMEM((rounds, 2 * fields * modes, totals), jnp.bfloat16),
             pltpu.SemaphoreType.DMA,
+            pltpu.SemaphoreType.DMA((4,)),
             pltpu.SemaphoreType.DMA((2,)),
             pltpu.SemaphoreType.DMA((2,)),
             pltpu.SemaphoreType.DMA((2,)),
         ],
         compiler_params=pltpu.CompilerParams(
-            collective_id=0, has_side_effects=True, vmem_limit_bytes=48 * 2**20
+            collective_id=0, has_side_effects=True, vmem_limit_bytes=63 * 2**20
         ),
     )(grid_rows, legendre_basis, owner_list, wave_speed)
     balanced = spectra.reshape(rounds, 2, fields, modes, totals)

time: 25.4 us -> 24.9 us (0.980)
  local copies, waits for them, and re-layouts: 5.86 us -> 5.48 us
    unnamed x6 -> x0, local copies, waits for them, and re-layouts: 2.77 us -> none
    pad x1, local copies, waits for them, and re-layouts: 1.63 us -> 2.59 us  [per_device(): balanced = jnp.pad(balanced, ((0, slots - rounds),) + ((0, 0),) * 4)]
    reshape x1, local copies, waits for them, and re-layouts: 0.66 us -> 1.46 us  [per_device(): rows.reshape(pairs, hemis, fields, modes, padded)]
    transpose x1, local copies, waits for them, and re-layouts: 0.81 us -> 1.43 us  [per_device(): grid_rows = jnp.transpose(grid_fields, (2, 3, 0, 1, 4)).reshape(-1, padded)]
where the time goes in v2:
time: 24.9 us; the launch traced here: 24.6 us
  Pallas kernels  18.5 us (74%)
  local copies, waits for them, and re-layouts  5.48 us (22%)
  between operations  0.64 us (3%)
    pallas_call x1, Pallas kernels, per_device(): pl.pallas_call(functools.partial(kernel, sizes), out_shape=(jax.ShapeDtyp...  18.5 us
    pad x1, local copies, waits for them, and re-layouts, per_device(): balanced = jnp.pad(balanced, ((0, slots - rounds),) + ((0, 0),) * 4)  2.59 us
    reshape x1, local copies, waits for them, and re-layouts, per_device(): rows.reshape(pairs, hemis, fields, modes, padded)  1.46 us
    transpose x1, local copies, waits for them, and re-layouts, per_device(): grid_rows = jnp.transpose(grid_fields, (2, 3, 0, 1, 4)).reshape(-1, padded)  1.43 us

profile of v2, /device:TPU:0, one launch (start us, length us, event | category | flops | bytes accessed | tf_op | source)
XLA Modules:
  0.0 24.6 jit_solution(17247980421359730578)
XLA Ops:
  0.6 1.4 %copy.6 = bf16[2,2,3,8,256]{4,3,2,1,0:T(8,128)(2,1)} copy(bf16[2,2,3,8,256]{4,1,0,3,2:T(2,128)(2,1)} %bitcast.9) | data formatting | bytes 98304 | tf_op jit(solution)/shard_map/transpose | solution.py:305
  2.1 18.5 %shard_map.59 = (bf16[5,48,640]{2,1,0:T(8,128)(2,1)}, bf16[96,256]{1,0:T(8,128)(2,1)}) custom-call(bf16[96,256]{1,0:T(8,128)(2,1)} %bitcast.8, bf16[40,1,32,640]{3,2,1,0:T(8,128)(2,1)} %basis_ref.1, s32[640]{0:T(1024)} %owner_hbm.1, f32[8]{0:T(128)} %speed_hbm.1), custom_call_target="tpu_custom_call" | custom-call | tf_op jit(solution)/shard_map/pallas_call | solution.py:307
  20.5 1.5 %copy.9 = bf16[2,2,3,8,256]{4,1,0,3,2:T(2,128)(2,1)} copy(bf16[2,2,3,8,256]{4,3,2,1,0:T(8,128)(2,1)} %bitcast.11) | data formatting | bytes 98304 | tf_op jit(solution)/shard_map/reshape | solution.py:344
  22.0 2.6 %pad.4 = bf16[40,2,3,8,640]{4,3,2,1,0:T(8,128)(2,1)} pad(bf16[5,2,3,8,640]{4,3,2,1,0:T(8,128)(2,1)} %bitcast.7, bf16[]{:T(256)} %constant.2.clone.1), padding=0_35x0_0x0_0x0_0x0_0 | pad | bytes 2764802 | tf_op jit(solution)/shard_map/jit(_pad)/pad | solution.py:342

commit v3 on v2

--- a/solution.py
+++ b/solution.py
@@ -40,11 +40,11 @@
 
 def kernel(
     sizes,
-    rows_hbm,
+    rows_ref,
     basis_ref,
     owner_hbm,
     speed_hbm,
-    spectra_hbm,
+    spectra_ref,
     grid_ref,
     table,
     basis,
@@ -53,10 +53,8 @@
     backward_out,
     backward_in,
     by_round,
-    rows_ref,
     owner_ref,
     speed_ref,
-    spectra_ref,
     own_sem,
     local_sems,
     basis_sems,
@@ -78,11 +76,8 @@
     )
     owner_copy = pltpu.make_async_copy(owner_hbm, owner_ref, local_sems.at[0])
     speed_copy = pltpu.make_async_copy(speed_hbm, speed_ref, local_sems.at[1])
-    rows_copy = pltpu.make_async_copy(rows_hbm, rows_ref, local_sems.at[2])
-    spectra_copy = pltpu.make_async_copy(spectra_ref, spectra_hbm, local_sems.at[3])
     owner_copy.start()
     speed_copy.start()
-    rows_copy.start()
     own_copy.start()
 
     barrier = pltpu.get_barrier_semaphore()
@@ -130,7 +125,6 @@
 
     owner_copy.wait()
     lax.fori_loop(0, ranks // together, fill, 0, unroll=2)
-    rows_copy.wait()
 
     blocks = []
     width = halves * inner
@@ -260,7 +254,6 @@
 
     backward_out[...] = by_round[...].astype(jnp.bfloat16).reshape(backward_out.shape)
     send(backward_out, backward_in, backward_sems)
-    spectra_copy.start()
     wait(backward_in, backward_sems.at[1])
 
     for pair in range(pairs):
@@ -284,7 +277,6 @@
                 (width, grid_ref.shape[1] - columns), jnp.bfloat16
             )
 
-    spectra_copy.wait()
     basis_copy.wait_send()
     wait(forward_out, forward_sems.at[0])
     wait(backward_out, backward_sems.at[0])
@@ -307,14 +299,12 @@
     spectra, rows = pl.pallas_call(
         functools.partial(kernel, sizes),
         out_shape=(
-            jax.ShapeDtypeStruct((rounds, 2 * fields * modes, totals), jnp.bfloat16),
-            jax.ShapeDtypeStruct(grid_rows.shape, jnp.bfloat16),
+            pltpu.VMEM((rounds, 2 * fields * modes, totals), jnp.bfloat16),
+            pltpu.VMEM(grid_rows.shape, jnp.bfloat16),
         ),
-        in_specs=[pl.BlockSpec(memory_space=pltpu.HBM)] * 4,
-        out_specs=[
-            pl.BlockSpec(memory_space=pltpu.HBM),
-            pl.BlockSpec(memory_space=pltpu.VMEM),
-        ],
+        in_specs=[pl.BlockSpec(memory_space=pltpu.VMEM)]
+        + [pl.BlockSpec(memory_space=pltpu.HBM)] * 3,
+        out_specs=[pl.BlockSpec(memory_space=pltpu.VMEM)] * 2,
         scratch_shapes=[
             pltpu.VMEM((pairs, ranks * padded_rounds, 2 * columns), jnp.bfloat16),
             pltpu.VMEM((hemis, rounds, half_count, totals), jnp.bfloat16),
@@ -323,20 +313,24 @@
             block,
             block,
             pltpu.VMEM((ranks * block_rows, lanes), jnp.float32),
-            pltpu.VMEM(grid_rows.shape, jnp.bfloat16),
             pltpu.SMEM(owner_list.shape, jnp.int32),
             pltpu.SMEM(wave_speed.shape, jnp.float32),
-            pltpu.VMEM((rounds, 2 * fields * modes, totals), jnp.bfloat16),
             pltpu.SemaphoreType.DMA,
-            pltpu.SemaphoreType.DMA((4,)),
+            pltpu.SemaphoreType.DMA((2,)),
             pltpu.SemaphoreType.DMA((2,)),
             pltpu.SemaphoreType.DMA((2,)),
             pltpu.SemaphoreType.DMA((2,)),
         ],
         compiler_params=pltpu.CompilerParams(
-            collective_id=0, has_side_effects=True, vmem_limit_bytes=63 * 2**20
+            collective_id=0, has_side_effects=True, vmem_limit_bytes=48 * 2**20
         ),
-    )(grid_rows, legendre_basis, owner_list, wave_speed)
+    )(
+        pltpu.with_memory_space_constraint(grid_rows, pltpu.VMEM),
+        *(
+            pltpu.with_memory_space_constraint(operand, pltpu.HBM)
+            for operand in (legendre_basis, owner_list, wave_speed)
+        ),
+    )
     balanced = spectra.reshape(rounds, 2, fields, modes, totals)
     if rounds < slots:
         balanced = jnp.pad(balanced, ((0, slots - rounds),) + ((0, 0),) * 4)

time: 24.9 us -> 21.8 us (0.88)
  local copies, waits for them, and re-layouts: 5.48 us -> 3.09 us
  Pallas kernels: 18.5 us -> 17.9 us
    pad x1, local copies, waits for them, and re-layouts: 2.59 us -> 1.63 us  [per_device(): balanced = jnp.pad(balanced, ((0, slots - rounds),) + ((0, 0),) * 4)]
    reshape x1, local copies, waits for them, and re-layouts: 1.46 us -> 0.66 us  [per_device(): rows.reshape(pairs, hemis, fields, modes, padded)]
    pallas_call x1, Pallas kernels: 18.5 us -> 17.9 us  [per_device(): pl.pallas_call(functools.partial(kernel, sizes), out_shape=(pltpu.VMEM((r...]
    transpose x1, local copies, waits for them, and re-layouts: 1.43 us -> 0.81 us  [per_device(): grid_rows = jnp.transpose(grid_fields, (2, 3, 0, 1, 4)).reshape(-1, padded)]
where the time goes in v3:
time: 21.8 us; the launch traced here: 21.6 us
  Pallas kernels  17.9 us (82%)
  local copies, waits for them, and re-layouts  3.09 us (14%)
  between operations  0.64 us (3%)
    pallas_call x1, Pallas kernels, per_device(): pl.pallas_call(functools.partial(kernel, sizes), out_shape=(pltpu.VMEM((r...  17.9 us
    pad x1, local copies, waits for them, and re-layouts, per_device(): balanced = jnp.pad(balanced, ((0, slots - rounds),) + ((0, 0),) * 4)  1.63 us
    transpose x1, local copies, waits for them, and re-layouts, per_device(): grid_rows = jnp.transpose(grid_fields, (2, 3, 0, 1, 4)).reshape(-1, padded)  0.81 us
    reshape x1, local copies, waits for them, and re-layouts, per_device(): rows.reshape(pairs, hemis, fields, modes, padded)  0.66 us

profile of v3, /device:TPU:0, one launch (start us, length us, event | category | flops | bytes accessed | tf_op | source)
XLA Modules:
  0.0 21.6 jit_solution(9300010824847254685)
XLA Ops:
  0.6 0.8 %copy.6 = bf16[2,2,3,8,256]{4,3,2,1,0:T(8,128)(2,1)S(1)} copy(bf16[2,2,3,8,256]{4,1,0,3,2:T(2,128)(2,1)} %bitcast.10) | data formatting | bytes 98304 | tf_op jit(solution)/shard_map/transpose | solution.py:297
  1.4 17.9 %shard_map.59 = (bf16[5,48,640]{2,1,0:T(8,128)(2,1)S(1)}, bf16[96,256]{1,0:T(8,128)(2,1)S(1)}) custom-call(bf16[96,256]{1,0:T(8,128)(2,1)S(1)} %bitcast.8, bf16[40,1,32,640]{3,2,1,0:T(8,128)(2,1)} %basis_ref.1, s32[640]{0:T(1024)} %owner_hbm.1, f32[8]{0:T(128)} %speed_hbm.1), custom_call_target="tpu_custom_call" | custom-call | tf_op jit(solution)/shard_map/pallas_call | solution.py:299
  19.3 0.7 %copy.9 = bf16[2,2,3,8,256]{4,1,0,3,2:T(2,128)(2,1)} copy(bf16[2,2,3,8,256]{4,3,2,1,0:T(8,128)(2,1)S(1)} %bitcast.9) | data formatting | bytes 98304 | tf_op jit(solution)/shard_map/reshape | solution.py:338
  20.0 1.6 %pad.4 = bf16[40,2,3,8,640]{4,3,2,1,0:T(8,128)(2,1)} pad(bf16[5,2,3,8,640]{4,3,2,1,0:T(8,128)(2,1)S(1)} %bitcast.7, bf16[]{:T(256)} %constant.2.clone.1), padding=0_35x0_0x0_0x0_0x0_0 | pad | bytes 2764802 | tf_op jit(solution)/shard_map/jit(_pad)/pad | solution.py:336

commit v4 on v3

--- a/solution.py
+++ b/solution.py
@@ -47,6 +47,7 @@
     spectra_ref,
     grid_ref,
     table,
+    placing,
     basis,
     forward_out,
     forward_in,
@@ -58,18 +59,25 @@
     own_sem,
     local_sems,
     basis_sems,
-    forward_sems,
-    backward_sems,
+    all_sems,
+    few_sems,
 ):
-    (ranks, halves, slots, rounds, padded_rounds, fields, modes, pairs, wave_count) = sizes
+    (ranks, halves, slots, rounds, fields, modes, pairs, wave_count) = sizes
     inner = fields * modes
+    width = halves * inner
     half_count = ranks * pairs
-    columns = table.shape[2] // 2
-    block_rows = pairs * padded_rounds
+    waves, columns = table.shape[1], table.shape[2] // 2
+    lanes = by_round.shape[1]
+    pieces = forward_out.shape[0]
+    per_piece = 8 // pairs
     totals = basis.shape[3]
     me = lax.axis_index("lat")
     hemisphere = lax.axis_index("fld")
     other = halves - 1 - hemisphere
+    reach = [
+        min(d for d in range(ranks) if largest(d * pairs + pairs - 1) >= g * per_piece * ranks)
+        for g in range(pieces)
+    ]
 
     own_copy = pltpu.make_async_copy(
         basis_ref.at[pl.ds(0, rounds), 0], basis.at[hemisphere], own_sem
@@ -80,6 +88,10 @@
     speed_copy.start()
     own_copy.start()
 
+    for g in range(1, pieces):
+        forward_in[g] = jnp.zeros(forward_in.shape[1:], jnp.bfloat16)
+        backward_in[g] = jnp.zeros(backward_in.shape[1:], jnp.bfloat16)
+
     barrier = pltpu.get_barrier_semaphore()
 
     def greet(step, carry):
@@ -92,18 +104,13 @@
     lax.fori_loop(1, ranks, greet, 0)
     pl.semaphore_signal(barrier, inc=1, device_id=(me, other), device_id_type=MESH)
 
-    together = max(1, 16 // padded_rounds)
-    chunk = together * padded_rounds
+    chunk = 16
     row_index = lax.broadcasted_iota(jnp.int32, (chunk, columns), 0)
     column = lax.broadcasted_iota(jnp.int32, (chunk, columns), 1)
     column_f = column.astype(jnp.float32)
 
     def fill(step, carry):
-        wave = jnp.full((chunk, columns), -1, jnp.int32)
-        for part in range(together):
-            for index in range(rounds):
-                number = owner_ref[(step * together + part) * slots + index]
-                wave = jnp.where(row_index == part * padded_rounds + index, number, wave)
+        wave = row_index + step * chunk
         product = wave.astype(jnp.float32) * column_f
         for pair in range(pairs):
             points = 20 + 4 * (me * pairs + pair)
@@ -114,8 +121,7 @@
             turns = jnp.floor(product * inverse + 0.5)
             angle = (product - turns * points_f) * inverse
             square = angle * angle
-            inside = (column < points) & (wave <= highest) & (wave >= 0)
-            scale = jnp.where(inside, scaling, 0.0)
+            scale = jnp.where((column < points) & (wave <= highest), scaling, 0.0)
             cosine = polynomial(COS_SERIES, square) * scale
             sine = polynomial(SIN_SERIES, square) * (angle * scale)
             where = pl.ds(pl.multiple_of(step * chunk, chunk), chunk)
@@ -123,50 +129,97 @@
             table[pair, where, columns : 2 * columns] = (-sine).astype(jnp.bfloat16)
         return carry
 
-    owner_copy.wait()
-    lax.fori_loop(0, ranks // together, fill, 0, unroll=2)
-
-    blocks = []
-    width = halves * inner
+    lax.fori_loop(0, waves // chunk, fill, 0, unroll=waves // chunk <= 8)
+
+    found = []
     for pair in range(pairs):
         values = rows_ref[pair * width : (pair + 1) * width, 0:columns]
         empty = jnp.zeros_like(values)
-        both = jnp.concatenate(
-            [
-                jnp.concatenate([values, empty], axis=1),
-                jnp.concatenate([empty, values], axis=1),
-            ],
-            axis=0,
-        )
-        found = lax.dot_general(
-            table[pair], both, (((1,), (1,)), ((), ())), preferred_element_type=jnp.float32
-        )
-        blocks.append(found.reshape(ranks, padded_rounds, 2 * width))
-    forward_out[:, :, 0 : 2 * width] = jnp.concatenate(blocks, axis=1).astype(jnp.bfloat16)
+        both = [
+            jnp.concatenate([values, empty], axis=1),
+            jnp.concatenate([empty, values], axis=1),
+        ]
+        if lanes > 2 * width:
+            both.append(jnp.zeros((lanes - 2 * width, 2 * columns), jnp.bfloat16))
+        found.append(
+            lax.dot_general(
+                table[pair],
+                jnp.concatenate(both, axis=0),
+                (((1,), (1,)), ((), ())),
+                preferred_element_type=jnp.float32,
+            ).astype(jnp.bfloat16)
+        )
+
+    owner_copy.wait()
+    place = lax.broadcasted_iota(jnp.int32, (8, waves), 0) % per_piece
+    natural = lax.broadcasted_iota(jnp.int32, (8, waves), 1)
+    for g in range(pieces):
+
+        def choose(device, carry, g=g):
+            wave = jnp.full((8, waves), -1, jnp.int32)
+            for index in range(min(per_piece, rounds - g * per_piece)):
+                number = owner_ref[device * slots + g * per_piece + index]
+                wave = jnp.where(place == index, number, wave)
+            where = pl.ds(pl.multiple_of((g * ranks + device) * 8, 8), 8)
+            placing[where, :] = jnp.where(wave == natural, 1.0, 0.0)
+            return carry
+
+        lax.fori_loop(0, ranks, choose, 0, unroll=ranks <= 16)
+    chosen = placing[...].astype(jnp.bfloat16)
+    placed = jnp.dot(
+        chosen, jnp.concatenate(found, axis=1), preferred_element_type=jnp.float32
+    )
+    block_rows = lax.broadcasted_iota(jnp.int32, (placed.shape[0], lanes), 0) % 8
+    outgoing = placed[:, 0:lanes]
+    for pair in range(1, pairs):
+        outgoing = jnp.where(
+            block_rows >= pair * per_piece,
+            placed[:, pair * lanes : (pair + 1) * lanes],
+            outgoing,
+        )
+    forward_out[...] = outgoing.reshape(forward_out.shape).astype(jnp.bfloat16)
 
     pl.semaphore_wait(barrier, ranks)
 
-    def send(out, into, sems):
+    def copy(out, into, g, peer, send_sem, recv_sem):
+        return pltpu.make_async_remote_copy(
+            src_ref=out.at[g, peer],
+            dst_ref=into.at[g, me],
+            send_sem=send_sem,
+            recv_sem=recv_sem,
+            device_id=(peer, hemisphere),
+            device_id_type=MESH,
+        )
+
+    def send_all(out, into, g, send_sem, recv_sem_of):
         def one(step, carry):
             peer = lax.rem(me + step, ranks)
-            pltpu.make_async_remote_copy(
-                src_ref=out.at[peer],
-                dst_ref=into.at[me],
-                send_sem=sems.at[0],
-                recv_sem=sems.at[1],
-                device_id=(peer, hemisphere),
-                device_id_type=MESH,
-            ).start()
+            copy(out, into, g, peer, send_sem, recv_sem_of).start()
             return carry
 
         lax.fori_loop(1, ranks, one, 0)
-        into[me] = out[me]
-
-    def wait(ref, sem):
-        part = ref.at[pl.ds(0, ranks - 1)]
+
+    def wait_all(ref, g, sem):
+        part = ref.at[g, pl.ds(0, ranks - 1)]
         pltpu.make_async_copy(part, part, sem).wait()
 
-    send(forward_out, forward_in, forward_sems)
+    def each_far(g, act):
+        def one(device, carry):
+            @pl.when(device != me)
+            def _():
+                act(device)
+
+            return carry
+
+        lax.fori_loop(reach[g], ranks, one, 0)
+
+    send_all(forward_out, forward_in, 0, all_sems.at[0, 0, 0], all_sems.at[0, 0, 1])
+    for g in range(1, pieces):
+
+        @pl.when(me >= reach[g])
+        def _(g=g):
+            send_all(forward_out, forward_in, g, all_sems.at[0, g, 0], few_sems.at[0, g, me])
+
     basis_copy = pltpu.make_async_remote_copy(
         src_ref=basis_ref.at[pl.ds(0, rounds), 0],
         dst_ref=basis.at[hemisphere],
@@ -176,6 +229,8 @@
         device_id_type=MESH,
     )
     basis_copy.start()
+    for g in range(pieces):
+        forward_in[g, me] = forward_out[g, me]
 
     speed_copy.wait()
     mode_index = lax.broadcasted_iota(jnp.int32, (modes, totals), 0)
@@ -189,14 +244,23 @@
     root_term = jnp.sqrt(stiffness)
     removed = stiffness * retained
 
-    wait(forward_in, forward_sems.at[1])
-    by_round[...] = forward_in[...].astype(jnp.float32).reshape(by_round.shape)
     own_copy.wait()
     basis_copy.wait_recv()
-
-    incoming = [
-        by_round[pl.ds(index, half_count, stride=padded_rounds), :] for index in range(rounds)
-    ]
+    wait_all(forward_in, 0, all_sems.at[0, 0, 1])
+    for g in range(1, pieces):
+        each_far(
+            g,
+            lambda device, g=g: pltpu.make_async_copy(
+                forward_in.at[g, device], forward_in.at[g, device], few_sems.at[0, g, device]
+            ).wait(),
+        )
+    by_round[...] = forward_in[...].astype(jnp.float32).reshape(by_round.shape)
+
+    def rows_of(index):
+        first = (index // per_piece) * ranks * 8 + index % per_piece
+        return pl.ds(first, half_count, stride=per_piece)
+
+    incoming = [by_round[rows_of(index), :] for index in range(rounds)]
     by_round[...] = jnp.zeros_like(by_round)
 
     for index in range(rounds):
@@ -215,7 +279,7 @@
                 coefficients, basis[side, index], preferred_element_type=jnp.float32
             )
         kept = degree_i >= number
-        pieces = []
+        values = []
         for part in range(2):
             first = part * inner
             vorticity = spectra[first : first + modes]
@@ -227,8 +291,8 @@
                 retained * divergence,
                 retained * geopotential - removed * rossby_part,
             ):
-                pieces.append(jnp.where(kept, value, 0.0))
-        balanced = jnp.concatenate(pieces, axis=0).astype(jnp.bfloat16)
+                values.append(jnp.where(kept, value, 0.0))
+        balanced = jnp.concatenate(values, axis=0).astype(jnp.bfloat16)
         spectra_ref[index] = balanced
         weight = jnp.where(number == 0, 1.0, 2.0)
         sides = [
@@ -245,29 +309,44 @@
             for part in range(2)
             for side in range(halves)
         ]
-        spare = by_round.shape[1] - 2 * width
-        if spare:
-            ordered.append(jnp.zeros((spare, half_count), jnp.float32))
-        by_round[pl.ds(index, half_count, stride=padded_rounds), :] = (
-            jnp.concatenate(ordered, axis=0).T * weight
-        )
-
-    backward_out[...] = by_round[...].astype(jnp.bfloat16).reshape(backward_out.shape)
-    send(backward_out, backward_in, backward_sems)
-    wait(backward_in, backward_sems.at[1])
-
+        if lanes > 2 * width:
+            ordered.append(jnp.zeros((lanes - 2 * width, half_count), jnp.float32))
+        by_round[rows_of(index), :] = jnp.concatenate(ordered, axis=0).T * weight
+
+    backward_out[...] = by_round[...].reshape(backward_out.shape).astype(jnp.bfloat16)
+    send_all(backward_out, backward_in, 0, all_sems.at[1, 0, 0], all_sems.at[1, 0, 1])
+    for g in range(1, pieces):
+        each_far(
+            g,
+            lambda device, g=g: copy(
+                backward_out, backward_in, g, device, few_sems.at[1, g, device], all_sems.at[1, g, 1]
+            ).start(),
+        )
+    for g in range(pieces):
+        backward_in[g, me] = backward_out[g, me]
+    wait_all(backward_in, 0, all_sems.at[1, 0, 1])
+    for g in range(1, pieces):
+
+        @pl.when(me >= reach[g])
+        def _(g=g):
+            wait_all(backward_in, g, all_sems.at[1, g, 1])
+
+    arrived = backward_in[...].astype(jnp.float32).reshape(by_round.shape).T
+    block_columns = lax.broadcasted_iota(jnp.int32, arrived.shape, 1) % 8
+    by_pair = [
+        jnp.where(block_columns // per_piece == pair, arrived, 0.0) for pair in range(pairs)
+    ]
+    ordered = jnp.dot(
+        jnp.concatenate(by_pair, axis=0).astype(jnp.bfloat16),
+        placing[...].astype(jnp.bfloat16),
+        preferred_element_type=jnp.float32,
+    )
     for pair in range(pairs):
-        first = pair * padded_rounds
-        arrived = (
-            backward_in[...]
-            .astype(jnp.float32)[:, first : first + padded_rounds]
-            .reshape(ranks * padded_rounds, by_round.shape[1])
-            .T
-        )
         result = jnp.zeros((width, columns), jnp.float32)
         for part in range(2):
+            first = pair * lanes + part * width
             result = result + jnp.dot(
-                arrived[part * width : (part + 1) * width].astype(jnp.bfloat16),
+                ordered[first : first + width].astype(jnp.bfloat16),
                 table[pair, :, part * columns : (part + 1) * columns],
                 preferred_element_type=jnp.float32,
             )
@@ -278,8 +357,24 @@
             )
 
     basis_copy.wait_send()
-    wait(forward_out, forward_sems.at[0])
-    wait(backward_out, backward_sems.at[0])
+    for way, out in ((0, forward_out), (1, backward_out)):
+        wait_all(out, 0, all_sems.at[way, 0, 0])
+    for g in range(1, pieces):
+
+        @pl.when(me >= reach[g])
+        def _(g=g):
+            wait_all(forward_out, g, all_sems.at[0, g, 0])
+
+        each_far(
+            g,
+            lambda device, g=g: pltpu.make_async_copy(
+                backward_out.at[g, device], backward_out.at[g, device], few_sems.at[1, g, device]
+            ).wait(),
+        )
+
+
+def largest(pair_index):
+    return (20 + 4 * pair_index - 1) // 2
 
 
 def per_device(ranks, halves, grid_fields, legendre_basis, owner_list, wave_speed):
@@ -287,15 +382,15 @@
     slots, _, half_count, totals = legendre_basis.shape
     wave_count = owner_list.shape[0]
     longest = 20 + 4 * (half_count - 1)
-    highest = min(wave_count - 1, (longest - 1) // 2)
+    highest = min(wave_count - 1, largest(half_count - 1))
     rounds = min(slots, highest // ranks + 1)
-    padded_rounds = round_up(rounds, 8)
+    pieces = round_up(rounds * pairs, 8) // 8
+    waves = rounds * ranks
     columns = min(padded, round_up(longest, 128))
     lanes = round_up(2 * hemis * fields * modes, 128)
-    block_rows = pairs * padded_rounds
-    sizes = (ranks, halves, slots, rounds, padded_rounds, fields, modes, pairs, wave_count)
+    sizes = (ranks, halves, slots, rounds, fields, modes, pairs, wave_count)
     grid_rows = jnp.transpose(grid_fields, (2, 3, 0, 1, 4)).reshape(-1, padded)
-    block = pltpu.VMEM((ranks, block_rows, lanes), jnp.bfloat16)
+    block = pltpu.VMEM((pieces, ranks, 8, lanes), jnp.bfloat16)
     spectra, rows = pl.pallas_call(
         functools.partial(kernel, sizes),
         out_shape=(
@@ -306,20 +401,21 @@
         + [pl.BlockSpec(memory_space=pltpu.HBM)] * 3,
         out_specs=[pl.BlockSpec(memory_space=pltpu.VMEM)] * 2,
         scratch_shapes=[
-            pltpu.VMEM((pairs, ranks * padded_rounds, 2 * columns), jnp.bfloat16),
+            pltpu.VMEM((pairs, waves, 2 * columns), jnp.bfloat16),
+            pltpu.VMEM((pieces * ranks * 8, waves), jnp.float32),
             pltpu.VMEM((hemis, rounds, half_count, totals), jnp.bfloat16),
             block,
             block,
             block,
             block,
-            pltpu.VMEM((ranks * block_rows, lanes), jnp.float32),
+            pltpu.VMEM((pieces * ranks * 8, lanes), jnp.float32),
             pltpu.SMEM(owner_list.shape, jnp.int32),
             pltpu.SMEM(wave_speed.shape, jnp.float32),
             pltpu.SemaphoreType.DMA,
             pltpu.SemaphoreType.DMA((2,)),
             pltpu.SemaphoreType.DMA((2,)),
-            pltpu.SemaphoreType.DMA((2,)),
-            pltpu.SemaphoreType.DMA((2,)),
+            pltpu.SemaphoreType.DMA((2, pieces, 2)),
+            pltpu.SemaphoreType.DMA((2, pieces, ranks)),
         ],
         compiler_params=pltpu.CompilerParams(
             collective_id=0, has_side_effects=True, vmem_limit_bytes=48 * 2**20

time: 21.8 us -> 22.2 us (1.018)
  Pallas kernels: 17.9 us -> 18.3 us
    pallas_call x1, Pallas kernels: 17.9 us -> 18.3 us  [per_device(): pl.pallas_call(functools.partial(kernel, sizes), out_shape=(pltpu.VMEM((r...]
where the time goes in v4:
time: 22.2 us; the launch traced here: 22.1 us
  Pallas kernels  18.3 us (82%)
  local copies, waits for them, and re-layouts  3.09 us (14%)
  between operations  0.64 us (3%)
    pallas_call x1, Pallas kernels, per_device(): pl.pallas_call(functools.partial(kernel, sizes), out_shape=(pltpu.VMEM((r...  18.3 us
    pad x1, local copies, waits for them, and re-layouts, per_device(): balanced = jnp.pad(balanced, ((0, slots - rounds),) + ((0, 0),) * 4)  1.63 us
    transpose x1, local copies, waits for them, and re-layouts, per_device(): grid_rows = jnp.transpose(grid_fields, (2, 3, 0, 1, 4)).reshape(-1, padded)  0.81 us
    reshape x1, local copies, waits for them, and re-layouts, per_device(): rows.reshape(pairs, hemis, fields, modes, padded)  0.66 us

profile of v4, /device:TPU:0, one launch (start us, length us, event | category | flops | bytes accessed | tf_op | source)
XLA Modules:
  0.0 22.1 jit_solution(13165393458255859736)
XLA Ops:
  0.6 0.8 %copy.6 = bf16[2,2,3,8,256]{4,3,2,1,0:T(8,128)(2,1)S(1)} copy(bf16[2,2,3,8,256]{4,1,0,3,2:T(2,128)(2,1)} %bitcast.10) | data formatting | bytes 98304 | tf_op jit(solution)/shard_map/transpose | solution.py:392
  1.4 18.3 %shard_map.59 = (bf16[5,48,640]{2,1,0:T(8,128)(2,1)S(1)}, bf16[96,256]{1,0:T(8,128)(2,1)S(1)}) custom-call(bf16[96,256]{1,0:T(8,128)(2,1)S(1)} %bitcast.8, bf16[40,1,32,640]{3,2,1,0:T(8,128)(2,1)} %basis_ref.1, s32[640]{0:T(1024)} %owner_hbm.1, f32[8]{0:T(128)} %speed_hbm.1), custom_call_target="tpu_custom_call" | custom-call | tf_op jit(solution)/shard_map/pallas_call | solution.py:394
  19.8 0.7 %copy.9 = bf16[2,2,3,8,256]{4,1,0,3,2:T(2,128)(2,1)} copy(bf16[2,2,3,8,256]{4,3,2,1,0:T(8,128)(2,1)S(1)} %bitcast.9) | data formatting | bytes 98304 | tf_op jit(solution)/shard_map/reshape | solution.py:434
  20.4 1.6 %pad.4 = bf16[40,2,3,8,640]{4,3,2,1,0:T(8,128)(2,1)} pad(bf16[5,2,3,8,640]{4,3,2,1,0:T(8,128)(2,1)S(1)} %bitcast.7, bf16[]{:T(256)} %constant.2.clone.1), padding=0_35x0_0x0_0x0_0x0_0 | pad | bytes 2764802 | tf_op jit(solution)/shard_map/jit(_pad)/pad | solution.py:432

commit v5 on v3

--- a/solution.py
+++ b/solution.py
@@ -40,13 +40,15 @@
 
 def kernel(
     sizes,
-    rows_ref,
+    grid_hbm,
     basis_ref,
     owner_hbm,
     speed_hbm,
     spectra_ref,
+    arrived_ref,
+    table,
     grid_ref,
-    table,
+    lines,
     basis,
     forward_out,
     forward_in,
@@ -65,32 +67,33 @@
     inner = fields * modes
     half_count = ranks * pairs
     columns = table.shape[2] // 2
-    block_rows = pairs * padded_rounds
     totals = basis.shape[3]
     me = lax.axis_index("lat")
     hemisphere = lax.axis_index("fld")
     other = halves - 1 - hemisphere
+
+    barrier = pltpu.get_barrier_semaphore()
+
+    def greet(step, carry):
+        peer = lax.rem(me + step, ranks)
+        pl.semaphore_signal(
+            barrier, inc=1, device_id=(peer, hemisphere), device_id_type=MESH
+        )
+        return carry
+
+    lax.fori_loop(1, ranks, greet, 0)
+    pl.semaphore_signal(barrier, inc=1, device_id=(me, other), device_id_type=MESH)
 
     own_copy = pltpu.make_async_copy(
         basis_ref.at[pl.ds(0, rounds), 0], basis.at[hemisphere], own_sem
     )
     owner_copy = pltpu.make_async_copy(owner_hbm, owner_ref, local_sems.at[0])
     speed_copy = pltpu.make_async_copy(speed_hbm, speed_ref, local_sems.at[1])
+    grid_copy = pltpu.make_async_copy(grid_hbm, grid_ref, local_sems.at[2])
     owner_copy.start()
+    grid_copy.start()
     speed_copy.start()
     own_copy.start()
-
-    barrier = pltpu.get_barrier_semaphore()
-
-    def greet(step, carry):
-        peer = lax.rem(me + step, ranks)
-        pl.semaphore_signal(
-            barrier, inc=1, device_id=(peer, hemisphere), device_id_type=MESH
-        )
-        return carry
-
-    lax.fori_loop(1, ranks, greet, 0)
-    pl.semaphore_signal(barrier, inc=1, device_id=(me, other), device_id_type=MESH)
 
     together = max(1, 16 // padded_rounds)
     chunk = together * padded_rounds
@@ -126,10 +129,26 @@
     owner_copy.wait()
     lax.fori_loop(0, ranks // together, fill, 0, unroll=2)
 
+    grid_copy.wait()
+    loaded = grid_ref[...].astype(jnp.float32).reshape(lines.shape[1], -1)
+    for tile in range(columns // 128):
+        lines[tile] = loaded[:, tile * 128 : (tile + 1) * 128]
     blocks = []
     width = halves * inner
     for pair in range(pairs):
-        values = rows_ref[pair * width : (pair + 1) * width, 0:columns]
+        values = jnp.concatenate(
+            [
+                jnp.concatenate(
+                    [
+                        lines[tile, pl.ds(pair * halves + side, inner, stride=pairs * halves), :]
+                        for tile in range(columns // 128)
+                    ],
+                    axis=1,
+                )
+                for side in range(halves)
+            ],
+            axis=0,
+        ).astype(jnp.bfloat16)
         empty = jnp.zeros_like(values)
         both = jnp.concatenate(
             [
@@ -256,12 +275,55 @@
     send(backward_out, backward_in, backward_sems)
     wait(backward_in, backward_sems.at[1])
 
+    arrived_ref[...] = backward_in[...]
+
+    basis_copy.wait_send()
+    wait(forward_out, forward_sems.at[0])
+    wait(backward_out, backward_sems.at[0])
+
+
+def finish(
+    sizes,
+    arrived_ref,
+    table,
+    spectra_ref,
+    balanced_hbm,
+    grid_hbm,
+    zeros,
+    lines,
+    grid_ref,
+    copy_sems,
+):
+    ranks, halves, slots, rounds, padded_rounds, inner, pairs = sizes
+    columns = table.shape[2] // 2
+    width = halves * inner
+    copies = [
+        pltpu.make_async_copy(
+            spectra_ref, balanced_hbm.at[pl.ds(0, rounds)], copy_sems.at[0]
+        )
+    ]
+    copies[0].start()
+    if rounds < slots:
+        zeros[...] = jnp.zeros_like(zeros)
+    for start in range(rounds, slots, rounds):
+        count = min(rounds, slots - start)
+        copies.append(
+            pltpu.make_async_copy(
+                zeros.at[pl.ds(0, count)],
+                balanced_hbm.at[pl.ds(start, count)],
+                copy_sems.at[len(copies)],
+            )
+        )
+        copies[-1].start()
+
+    for tile in range(columns // 128, lines.shape[0]):
+        lines[tile] = jnp.zeros(lines.shape[1:], jnp.float32)
     for pair in range(pairs):
         first = pair * padded_rounds
         arrived = (
-            backward_in[...]
+            arrived_ref[...]
             .astype(jnp.float32)[:, first : first + padded_rounds]
-            .reshape(ranks * padded_rounds, by_round.shape[1])
+            .reshape(ranks * padded_rounds, arrived_ref.shape[2])
             .T
         )
         result = jnp.zeros((width, columns), jnp.float32)
@@ -271,15 +333,18 @@
                 table[pair, :, part * columns : (part + 1) * columns],
                 preferred_element_type=jnp.float32,
             )
-        grid_ref[pair * width : (pair + 1) * width, 0:columns] = result.astype(jnp.bfloat16)
-        if columns < grid_ref.shape[1]:
-            grid_ref[pair * width : (pair + 1) * width, columns:] = jnp.zeros(
-                (width, grid_ref.shape[1] - columns), jnp.bfloat16
-            )
-
-    basis_copy.wait_send()
-    wait(forward_out, forward_sems.at[0])
-    wait(backward_out, backward_sems.at[0])
+        for side in range(halves):
+            where = pl.ds(pair * halves + side, inner, stride=pairs * halves)
+            for tile in range(columns // 128):
+                lines[tile, where, :] = result[
+                    side * inner : (side + 1) * inner, tile * 128 : (tile + 1) * 128
+                ]
+    joined = jnp.concatenate([lines[tile] for tile in range(lines.shape[0])], axis=1)
+    grid_ref[...] = joined.reshape(grid_ref.shape).astype(jnp.bfloat16)
+    copies.append(pltpu.make_async_copy(grid_ref, grid_hbm, copy_sems.at[len(copies)]))
+    copies[-1].start()
+    for one in copies:
+        one.wait()
 
 
 def per_device(ranks, halves, grid_fields, legendre_basis, owner_list, wave_speed):
@@ -294,19 +359,24 @@
     lanes = round_up(2 * hemis * fields * modes, 128)
     block_rows = pairs * padded_rounds
     sizes = (ranks, halves, slots, rounds, padded_rounds, fields, modes, pairs, wave_count)
-    grid_rows = jnp.transpose(grid_fields, (2, 3, 0, 1, 4)).reshape(-1, padded)
+    table_shape = (pairs, ranks * padded_rounds, 2 * columns)
     block = pltpu.VMEM((ranks, block_rows, lanes), jnp.bfloat16)
-    spectra, rows = pl.pallas_call(
+    line_scratch = [
+        pltpu.VMEM(grid_fields.shape, jnp.bfloat16),
+        pltpu.VMEM((padded // 128, fields * modes * pairs * hemis, 128), jnp.float32),
+    ]
+    spectra_shape = (rounds, 2 * fields * modes, totals)
+    spectra, arrived, table = pl.pallas_call(
         functools.partial(kernel, sizes),
         out_shape=(
-            pltpu.VMEM((rounds, 2 * fields * modes, totals), jnp.bfloat16),
-            pltpu.VMEM(grid_rows.shape, jnp.bfloat16),
-        ),
-        in_specs=[pl.BlockSpec(memory_space=pltpu.VMEM)]
-        + [pl.BlockSpec(memory_space=pltpu.HBM)] * 3,
-        out_specs=[pl.BlockSpec(memory_space=pltpu.VMEM)] * 2,
-        scratch_shapes=[
-            pltpu.VMEM((pairs, ranks * padded_rounds, 2 * columns), jnp.bfloat16),
+            pltpu.VMEM(spectra_shape, jnp.bfloat16),
+            block,
+            pltpu.VMEM(table_shape, jnp.bfloat16),
+        ),
+        in_specs=[pl.BlockSpec(memory_space=pltpu.HBM)] * 4,
+        out_specs=[pl.BlockSpec(memory_space=pltpu.VMEM)] * 3,
+        scratch_shapes=line_scratch
+        + [
             pltpu.VMEM((hemis, rounds, half_count, totals), jnp.bfloat16),
             block,
             block,
@@ -316,28 +386,42 @@
             pltpu.SMEM(owner_list.shape, jnp.int32),
             pltpu.SMEM(wave_speed.shape, jnp.float32),
             pltpu.SemaphoreType.DMA,
-            pltpu.SemaphoreType.DMA((2,)),
+            pltpu.SemaphoreType.DMA((3,)),
             pltpu.SemaphoreType.DMA((2,)),
             pltpu.SemaphoreType.DMA((2,)),
             pltpu.SemaphoreType.DMA((2,)),
         ],
         compiler_params=pltpu.CompilerParams(
-            collective_id=0, has_side_effects=True, vmem_limit_bytes=48 * 2**20
+            collective_id=0, has_side_effects=True, vmem_limit_bytes=40 * 2**20
         ),
     )(
-        pltpu.with_memory_space_constraint(grid_rows, pltpu.VMEM),
         *(
             pltpu.with_memory_space_constraint(operand, pltpu.HBM)
-            for operand in (legendre_basis, owner_list, wave_speed)
+            for operand in (grid_fields, legendre_basis, owner_list, wave_speed)
         ),
     )
-    balanced = spectra.reshape(rounds, 2, fields, modes, totals)
-    if rounds < slots:
-        balanced = jnp.pad(balanced, ((0, slots - rounds),) + ((0, 0),) * 4)
-    balanced_grid = jnp.transpose(
-        rows.reshape(pairs, hemis, fields, modes, padded), (2, 3, 0, 1, 4)
+    copies = 2 + -(-(slots - rounds) // rounds)
+    balanced, balanced_grid = pl.pallas_call(
+        functools.partial(
+            finish, (ranks, halves, slots, rounds, padded_rounds, fields * modes, pairs)
+        ),
+        out_shape=(
+            pltpu.HBM((slots,) + spectra_shape[1:], jnp.bfloat16),
+            pltpu.HBM(grid_fields.shape, jnp.bfloat16),
+        ),
+        in_specs=[pl.BlockSpec(memory_space=pltpu.VMEM)] * 3,
+        out_specs=[pl.BlockSpec(memory_space=pltpu.HBM)] * 2,
+        scratch_shapes=[pltpu.VMEM(spectra_shape, jnp.bfloat16)]
+        + line_scratch[::-1]
+        + [pltpu.SemaphoreType.DMA((copies,))],
+        compiler_params=pltpu.CompilerParams(vmem_limit_bytes=40 * 2**20),
+    )(
+        *(
+            pltpu.with_memory_space_constraint(operand, pltpu.VMEM)
+            for operand in (arrived, table, spectra)
+        ),
     )
-    return (balanced, balanced_grid)
+    return (balanced.reshape(slots, 2, fields, modes, totals), balanced_grid)
 
 
 def solution(mesh):

time: 21.8 us -> 20 us (0.917)
  local copies, waits for them, and re-layouts: 3.09 us -> 0 us
  Pallas kernels: 17.9 us -> 19.2 us
    pad x1 -> x0, local copies, waits for them, and re-layouts: 1.63 us -> none  [per_device(): balanced = jnp.pad(balanced, ((0, slots - rounds),) + ((0, 0),) * 4)]
    pallas_call x1 -> x2, Pallas kernels: 17.9 us -> 19.2 us  [the longest x1 17.6 us: per_device(): pl.pallas_call(functools.partial(kernel, sizes), out_shape=(pltpu.VMEM(sp...]
    transpose x1 -> x0, local copies, waits for them, and re-layouts: 0.81 us -> none  [per_device(): grid_rows = jnp.transpose(grid_fields, (2, 3, 0, 1, 4)).reshape(-1, padded)]
    reshape x1 -> x0, local copies, waits for them, and re-layouts: 0.66 us -> none  [per_device(): rows.reshape(pairs, hemis, fields, modes, padded)]
where the time goes in v5:
time: 20 us; the launch traced here: 19.8 us
  Pallas kernels  19.2 us (96%)
  between operations  0.64 us (3%)
    pallas_call x1, Pallas kernels, per_device(): pl.pallas_call(functools.partial(kernel, sizes), out_shape=(pltpu.VMEM(sp...  17.6 us
    pallas_call x1, Pallas kernels, per_device(): pl.pallas_call(functools.partial(finish, (ranks, halves, slots, rounds, p...  1.51 us

profile of v5, /device:TPU:0, one launch (start us, length us, event | category | flops | bytes accessed | tf_op | source)
XLA Modules:
  0.0 19.8 jit_solution(15386156542736695699)
XLA Ops:
  0.6 17.6 %shard_map.59 = (bf16[5,48,640]{2,1,0:T(8,128)(2,1)S(1)}, bf16[16,16,128]{2,1,0:T(8,128)(2,1)S(1)}, bf16[2,128,512]{2,1,0:T(8,128)(2,1)S(1)}) custom-call(bf16[3,8,2,2,256]{4,3,2,1,0:T(2,128)(2,1)} %grid_hbm.1, bf16[40,1,32,640]{3,2,1,0:T(8,128)(2,1)} %basis_ref.1, s32[640]{0:T(1024)} %owner_hbm.1, f32[8]{0:T(128)} %speed_hbm.1), custom_call_target="tpu_custom_call" | custom-call | tf_op jit(solution)/shard_map/pallas_call | solution.py:369
  18.3 1.5 %shard_map.60 = (bf16[40,48,640]{2,1,0:T(8,128)(2,1)}, bf16[3,8,2,2,256]{4,3,2,1,0:T(2,128)(2,1)}) custom-call(bf16[16,16,128]{2,1,0:T(8,128)(2,1)S(1)} %get-tuple-element.7.arrived_ref, bf16[2,128,512]{2,1,0:T(8,128)(2,1)S(1)} %get-tuple-element.8.table, bf16[5,48,640]{2,1,0:T(8,128)(2,1)S(1)} %get-tuple-element.9.spectra_ref), custom_call_target="tpu_custom_call" | custom-call | tf_op jit(solution)/shard_map/pallas_call | solution.py:404

commit v6 on v5

--- a/solution.py
+++ b/solution.py
@@ -36,6 +36,30 @@
 
 def round_up(value, multiple):
     return -(-value // multiple) * multiple
+
+
+def for_partners(me, ranks, act):
+    bits = ranks.bit_length() - 1
+    if ranks != 1 << bits:
+
+        def around(step, carry):
+            act(lax.rem(me + step, ranks))
+            return carry
+
+        lax.fori_loop(1, ranks, around, 0)
+        return
+    flips = [(1 - 2 * ((me // (1 << bit)) % 2)) * (1 << bit) for bit in range(bits)]
+    if ranks <= 16:
+        for step in range(ranks - 1, 0, -1):
+            act(me + sum(flips[bit] for bit in range(bits) if step >> bit & 1))
+        return
+
+    def across(index, carry):
+        step = ranks - 1 - index
+        act(me + sum(flips[bit] * ((step // (1 << bit)) % 2) for bit in range(bits)))
+        return carry
+
+    lax.fori_loop(0, ranks - 1, across, 0)
 
 
 def kernel(
@@ -67,25 +91,27 @@
     inner = fields * modes
     half_count = ranks * pairs
     columns = table.shape[2] // 2
-    totals = basis.shape[3]
+    totals = basis.shape[2]
     me = lax.axis_index("lat")
     hemisphere = lax.axis_index("fld")
     other = halves - 1 - hemisphere
 
     barrier = pltpu.get_barrier_semaphore()
 
-    def greet(step, carry):
-        peer = lax.rem(me + step, ranks)
-        pl.semaphore_signal(
+    for_partners(
+        me,
+        ranks,
+        lambda peer: pl.semaphore_signal(
             barrier, inc=1, device_id=(peer, hemisphere), device_id_type=MESH
-        )
-        return carry
-
-    lax.fori_loop(1, ranks, greet, 0)
+        ),
+    )
     pl.semaphore_signal(barrier, inc=1, device_id=(me, other), device_id_type=MESH)
 
+    own_side = basis.at[
+        :, pl.ds(pl.multiple_of(hemisphere * half_count, half_count), half_count)
+    ]
     own_copy = pltpu.make_async_copy(
-        basis_ref.at[pl.ds(0, rounds), 0], basis.at[hemisphere], own_sem
+        basis_ref.at[pl.ds(0, rounds), 0], own_side, own_sem
     )
     owner_copy = pltpu.make_async_copy(owner_hbm, owner_ref, local_sems.at[0])
     speed_copy = pltpu.make_async_copy(speed_hbm, speed_ref, local_sems.at[1])
@@ -166,8 +192,7 @@
     pl.semaphore_wait(barrier, ranks)
 
     def send(out, into, sems):
-        def one(step, carry):
-            peer = lax.rem(me + step, ranks)
+        def one(peer):
             pltpu.make_async_remote_copy(
                 src_ref=out.at[peer],
                 dst_ref=into.at[me],
@@ -176,9 +201,8 @@
                 device_id=(peer, hemisphere),
                 device_id_type=MESH,
             ).start()
-            return carry
-
-        lax.fori_loop(1, ranks, one, 0)
+
+        for_partners(me, ranks, one)
         into[me] = out[me]
 
     def wait(ref, sem):
@@ -188,7 +212,7 @@
     send(forward_out, forward_in, forward_sems)
     basis_copy = pltpu.make_async_remote_copy(
         src_ref=basis_ref.at[pl.ds(0, rounds), 0],
-        dst_ref=basis.at[hemisphere],
+        dst_ref=own_side,
         send_sem=basis_sems.at[0],
         recv_sem=basis_sems.at[1],
         device_id=(me, other),
@@ -221,18 +245,20 @@
     for index in range(rounds):
         number = owner_ref[me * slots + index]
         turned = incoming[index].T
-        spectra = jnp.zeros((2 * inner, totals), jnp.float32)
-        for side in range(halves):
-            coefficients = jnp.concatenate(
-                [
-                    turned[part * width + side * inner : part * width + (side + 1) * inner]
-                    for part in range(2)
-                ],
-                axis=0,
-            ).astype(jnp.bfloat16)
-            spectra = spectra + jnp.dot(
-                coefficients, basis[side, index], preferred_element_type=jnp.float32
-            )
+        coefficients = jnp.concatenate(
+            [
+                jnp.concatenate(
+                    [
+                        turned[part * width + side * inner : part * width + (side + 1) * inner]
+                        for part in range(2)
+                    ],
+                    axis=0,
+                )
+                for side in range(halves)
+            ],
+            axis=1,
+        ).astype(jnp.bfloat16)
+        spectra = jnp.dot(coefficients, basis[index], preferred_element_type=jnp.float32)
         kept = degree_i >= number
         pieces = []
         for part in range(2):
@@ -250,17 +276,13 @@
         balanced = jnp.concatenate(pieces, axis=0).astype(jnp.bfloat16)
         spectra_ref[index] = balanced
         weight = jnp.where(number == 0, 1.0, 2.0)
-        sides = [
-            lax.dot_general(
-                balanced,
-                basis[side, index],
-                (((1,), (1,)), ((), ())),
-                preferred_element_type=jnp.float32,
-            )
-            for side in range(halves)
-        ]
+        returned = lax.dot_general(
+            balanced, basis[index], (((1,), (1,)), ((), ())), preferred_element_type=jnp.float32
+        )
         ordered = [
-            sides[side][part * inner : (part + 1) * inner]
+            returned[
+                part * inner : (part + 1) * inner, side * half_count : (side + 1) * half_count
+            ]
             for part in range(2)
             for side in range(halves)
         ]
@@ -377,7 +399,7 @@
         out_specs=[pl.BlockSpec(memory_space=pltpu.VMEM)] * 3,
         scratch_shapes=line_scratch
         + [
-            pltpu.VMEM((hemis, rounds, half_count, totals), jnp.bfloat16),
+            pltpu.VMEM((rounds, hemis * half_count, totals), jnp.bfloat16),
             block,
             block,
             block,

time: 20 us -> 19.1 us (0.955)
  Pallas kernels: 19.2 us -> 18.3 us
    pallas_call x1, Pallas kernels: 17.6 us -> 16.8 us  [per_device(): pl.pallas_call(functools.partial(kernel, sizes), out_shape=(pltpu.VMEM(sp...]
where the time goes in v6:
time: 19.1 us; the launch traced here: 19 us
  Pallas kernels  18.3 us (96%)
  between operations  0.64 us (3%)
    pallas_call x1, Pallas kernels, per_device(): pl.pallas_call(functools.partial(kernel, sizes), out_shape=(pltpu.VMEM(sp...  16.8 us
    pallas_call x1, Pallas kernels, per_device(): pl.pallas_call(functools.partial(finish, (ranks, halves, slots, rounds, p...  1.51 us

profile of v6, /device:TPU:0, one launch (start us, length us, event | category | flops | bytes accessed | tf_op | source)
XLA Modules:
  0.0 19.0 jit_solution(1320630405052420736)
XLA Ops:
  0.6 16.8 %shard_map.59 = (bf16[5,48,640]{2,1,0:T(8,128)(2,1)S(1)}, bf16[16,16,128]{2,1,0:T(8,128)(2,1)S(1)}, bf16[2,128,512]{2,1,0:T(8,128)(2,1)S(1)}) custom-call(bf16[3,8,2,2,256]{4,3,2,1,0:T(2,128)(2,1)} %grid_hbm.1, bf16[40,1,32,640]{3,2,1,0:T(8,128)(2,1)} %basis_ref.1, s32[640]{0:T(1024)} %owner_hbm.1, f32[8]{0:T(128)} %speed_hbm.1), custom_call_target="tpu_custom_call" | custom-call | tf_op jit(solution)/shard_map/pallas_call | solution.py:391
  17.4 1.5 %shard_map.60 = (bf16[40,48,640]{2,1,0:T(8,128)(2,1)}, bf16[3,8,2,2,256]{4,3,2,1,0:T(2,128)(2,1)}) custom-call(bf16[16,16,128]{2,1,0:T(8,128)(2,1)S(1)} %get-tuple-element.7.arrived_ref, bf16[2,128,512]{2,1,0:T(8,128)(2,1)S(1)} %get-tuple-element.8.table, bf16[5,48,640]{2,1,0:T(8,128)(2,1)S(1)} %get-tuple-element.9.spectra_ref), custom_call_target="tpu_custom_call" | custom-call | tf_op jit(solution)/shard_map/pallas_call | solution.py:426

commit v7 on v6

--- a/solution.py
+++ b/solution.py
@@ -79,6 +79,7 @@
     backward_out,
     backward_in,
     by_round,
+    outgoing,
     owner_ref,
     speed_ref,
     own_sem,
@@ -232,6 +233,9 @@
     root_term = jnp.sqrt(stiffness)
     removed = stiffness * retained
 
+    numbers = [owner_ref[me * slots + index] for index in range(rounds)]
+    outgoing[...] = jnp.zeros_like(outgoing)
+
     wait(forward_in, forward_sems.at[1])
     by_round[...] = forward_in[...].astype(jnp.float32).reshape(by_round.shape)
     own_copy.wait()
@@ -240,16 +244,13 @@
     incoming = [
         by_round[pl.ds(index, half_count, stride=padded_rounds), :] for index in range(rounds)
     ]
-    by_round[...] = jnp.zeros_like(by_round)
-
-    for index in range(rounds):
-        number = owner_ref[me * slots + index]
-        turned = incoming[index].T
-        coefficients = jnp.concatenate(
+    turned = [rows.T for rows in incoming]
+    coefficients = [
+        jnp.concatenate(
             [
                 jnp.concatenate(
                     [
-                        turned[part * width + side * inner : part * width + (side + 1) * inner]
+                        rows[part * width + side * inner : part * width + (side + 1) * inner]
                         for part in range(2)
                     ],
                     axis=0,
@@ -258,14 +259,21 @@
             ],
             axis=1,
         ).astype(jnp.bfloat16)
-        spectra = jnp.dot(coefficients, basis[index], preferred_element_type=jnp.float32)
-        kept = degree_i >= number
+        for rows in turned
+    ]
+    spectra = [
+        jnp.dot(rows, basis[index], preferred_element_type=jnp.float32)
+        for index, rows in enumerate(coefficients)
+    ]
+    balanced = []
+    for index, rows in enumerate(spectra):
+        kept = degree_i >= numbers[index]
         pieces = []
         for part in range(2):
             first = part * inner
-            vorticity = spectra[first : first + modes]
-            divergence = spectra[first + modes : first + 2 * modes]
-            geopotential = spectra[first + 2 * modes : first + 3 * modes]
+            vorticity = rows[first : first + modes]
+            divergence = rows[first + modes : first + 2 * modes]
+            geopotential = rows[first + 2 * modes : first + 3 * modes]
             rossby_part = (root_term * vorticity - geopotential) * retained
             for value in (
                 retained * vorticity + removed * root_term * rossby_part,
@@ -273,28 +281,31 @@
                 retained * geopotential - removed * rossby_part,
             ):
                 pieces.append(jnp.where(kept, value, 0.0))
-        balanced = jnp.concatenate(pieces, axis=0).astype(jnp.bfloat16)
-        spectra_ref[index] = balanced
-        weight = jnp.where(number == 0, 1.0, 2.0)
-        returned = lax.dot_general(
-            balanced, basis[index], (((1,), (1,)), ((), ())), preferred_element_type=jnp.float32
-        )
+        balanced.append(jnp.concatenate(pieces, axis=0).astype(jnp.bfloat16))
+    returned = [
+        lax.dot_general(
+            rows, basis[index], (((1,), (1,)), ((), ())), preferred_element_type=jnp.float32
+        )
+        for index, rows in enumerate(balanced)
+    ]
+    spare = by_round.shape[1] - 2 * width
+    for index, rows in enumerate(returned):
         ordered = [
-            returned[
-                part * inner : (part + 1) * inner, side * half_count : (side + 1) * half_count
-            ]
+            rows[part * inner : (part + 1) * inner, side * half_count : (side + 1) * half_count]
             for part in range(2)
             for side in range(halves)
         ]
-        spare = by_round.shape[1] - 2 * width
         if spare:
             ordered.append(jnp.zeros((spare, half_count), jnp.float32))
-        by_round[pl.ds(index, half_count, stride=padded_rounds), :] = (
+        weight = jnp.where(numbers[index] == 0, 1.0, 2.0)
+        outgoing[pl.ds(index, half_count, stride=padded_rounds), :] = (
             jnp.concatenate(ordered, axis=0).T * weight
         )
 
-    backward_out[...] = by_round[...].astype(jnp.bfloat16).reshape(backward_out.shape)
+    backward_out[...] = outgoing[...].astype(jnp.bfloat16).reshape(backward_out.shape)
     send(backward_out, backward_in, backward_sems)
+    for index, rows in enumerate(balanced):
+        spectra_ref[index] = rows
     wait(backward_in, backward_sems.at[1])
 
     arrived_ref[...] = backward_in[...]
@@ -405,6 +416,7 @@
             block,
             block,
             pltpu.VMEM((ranks * block_rows, lanes), jnp.float32),
+            pltpu.VMEM((ranks * block_rows, lanes), jnp.float32),
             pltpu.SMEM(owner_list.shape, jnp.int32),
             pltpu.SMEM(wave_speed.shape, jnp.float32),
             pltpu.SemaphoreType.DMA,

time: 19.1 us -> 19 us (level)
  no operation moved by 1% of the time
where the time goes in v7:
time: 19 us; the launch traced here: 18.8 us
  Pallas kernels  18.2 us (96%)
  between operations  0.64 us (3%)
    pallas_call x1, Pallas kernels, per_device(): pl.pallas_call(functools.partial(kernel, sizes), out_shape=(pltpu.VMEM(sp...  16.7 us
    pallas_call x1, Pallas kernels, per_device(): pl.pallas_call(functools.partial(finish, (ranks, halves, slots, rounds, p...  1.51 us

profile of v7, /device:TPU:0, one launch (start us, length us, event | category | flops | bytes accessed | tf_op | source)
XLA Modules:
  0.0 18.8 jit_solution(8670615600600011124)
XLA Ops:
  0.6 16.7 %shard_map.59 = (bf16[5,48,640]{2,1,0:T(8,128)(2,1)S(1)}, bf16[16,16,128]{2,1,0:T(8,128)(2,1)S(1)}, bf16[2,128,512]{2,1,0:T(8,128)(2,1)S(1)}) custom-call(bf16[3,8,2,2,256]{4,3,2,1,0:T(2,128)(2,1)} %grid_hbm.1, bf16[40,1,32,640]{3,2,1,0:T(8,128)(2,1)} %basis_ref.1, s32[640]{0:T(1024)} %owner_hbm.1, f32[8]{0:T(128)} %speed_hbm.1), custom_call_target="tpu_custom_call" | custom-call | tf_op jit(solution)/shard_map/pallas_call | solution.py:402
  17.3 1.5 %shard_map.60 = (bf16[40,48,640]{2,1,0:T(8,128)(2,1)}, bf16[3,8,2,2,256]{4,3,2,1,0:T(2,128)(2,1)}) custom-call(bf16[16,16,128]{2,1,0:T(8,128)(2,1)S(1)} %get-tuple-element.7.arrived_ref, bf16[2,128,512]{2,1,0:T(8,128)(2,1)S(1)} %get-tuple-element.8.table, bf16[5,48,640]{2,1,0:T(8,128)(2,1)S(1)} %get-tuple-element.9.spectra_ref), custom_call_target="tpu_custom_call" | custom-call | tf_op jit(solution)/shard_map/pallas_call | solution.py:438

commit v8 on v7

--- a/solution.py
+++ b/solution.py
@@ -210,9 +210,9 @@
         part = ref.at[pl.ds(0, ranks - 1)]
         pltpu.make_async_copy(part, part, sem).wait()
 
-    send(forward_out, forward_in, forward_sems)
+    own_copy.wait()
     basis_copy = pltpu.make_async_remote_copy(
-        src_ref=basis_ref.at[pl.ds(0, rounds), 0],
+        src_ref=own_side,
         dst_ref=own_side,
         send_sem=basis_sems.at[0],
         recv_sem=basis_sems.at[1],
@@ -220,6 +220,7 @@
         device_id_type=MESH,
     )
     basis_copy.start()
+    send(forward_out, forward_in, forward_sems)
 
     speed_copy.wait()
     mode_index = lax.broadcasted_iota(jnp.int32, (modes, totals), 0)
@@ -238,7 +239,6 @@
 
     wait(forward_in, forward_sems.at[1])
     by_round[...] = forward_in[...].astype(jnp.float32).reshape(by_round.shape)
-    own_copy.wait()
     basis_copy.wait_recv()
 
     incoming = [

time: 19 us -> 19 us (level)
  no operation moved by 1% of the time
where the time goes in v8:
time: 19 us; the launch traced here: 18.8 us
  Pallas kernels  18.2 us (96%)
  between operations  0.64 us (3%)
    pallas_call x1, Pallas kernels, per_device(): pl.pallas_call(functools.partial(kernel, sizes), out_shape=(pltpu.VMEM(sp...  16.7 us
    pallas_call x1, Pallas kernels, per_device(): pl.pallas_call(functools.partial(finish, (ranks, halves, slots, rounds, p...  1.51 us

profile of v8, /device:TPU:0, one launch (start us, length us, event | category | flops | bytes accessed | tf_op | source)
XLA Modules:
  0.0 18.8 jit_solution(11090420668121453713)
XLA Ops:
  0.6 16.7 %shard_map.59 = (bf16[5,48,640]{2,1,0:T(8,128)(2,1)S(1)}, bf16[16,16,128]{2,1,0:T(8,128)(2,1)S(1)}, bf16[2,128,512]{2,1,0:T(8,128)(2,1)S(1)}) custom-call(bf16[3,8,2,2,256]{4,3,2,1,0:T(2,128)(2,1)} %grid_hbm.1, bf16[40,1,32,640]{3,2,1,0:T(8,128)(2,1)} %basis_ref.1, s32[640]{0:T(1024)} %owner_hbm.1, f32[8]{0:T(128)} %speed_hbm.1), custom_call_target="tpu_custom_call" | custom-call | tf_op jit(solution)/shard_map/pallas_call | solution.py:402
  17.3 1.5 %shard_map.60 = (bf16[40,48,640]{2,1,0:T(8,128)(2,1)}, bf16[3,8,2,2,256]{4,3,2,1,0:T(2,128)(2,1)}) custom-call(bf16[16,16,128]{2,1,0:T(8,128)(2,1)S(1)} %get-tuple-element.7.arrived_ref, bf16[2,128,512]{2,1,0:T(8,128)(2,1)S(1)} %get-tuple-element.8.table, bf16[5,48,640]{2,1,0:T(8,128)(2,1)S(1)} %get-tuple-element.9.spectra_ref), custom_call_target="tpu_custom_call" | custom-call | tf_op jit(solution)/shard_map/pallas_call | solution.py:438

commit v9 on v8

--- a/solution.py
+++ b/solution.py
@@ -124,16 +124,17 @@
 
     together = max(1, 16 // padded_rounds)
     chunk = together * padded_rounds
-    row_index = lax.broadcasted_iota(jnp.int32, (chunk, columns), 0)
+    row_index = lax.broadcasted_iota(jnp.int32, (chunk, 128), 0)
     column = lax.broadcasted_iota(jnp.int32, (chunk, columns), 1)
     column_f = column.astype(jnp.float32)
 
     def fill(step, carry):
-        wave = jnp.full((chunk, columns), -1, jnp.int32)
+        wave = jnp.full((chunk, 128), -1, jnp.int32)
         for part in range(together):
             for index in range(rounds):
                 number = owner_ref[(step * together + part) * slots + index]
                 wave = jnp.where(row_index == part * padded_rounds + index, number, wave)
+        wave = jnp.concatenate([wave] * (columns // 128), axis=1)
         product = wave.astype(jnp.float32) * column_f
         for pair in range(pairs):
             points = 20 + 4 * (me * pairs + pair)
@@ -154,7 +155,7 @@
         return carry
 
     owner_copy.wait()
-    lax.fori_loop(0, ranks // together, fill, 0, unroll=2)
+    lax.fori_loop(0, ranks // together, fill, 0, unroll=8 if ranks <= 16 else 1)
 
     grid_copy.wait()
     loaded = grid_ref[...].astype(jnp.float32).reshape(lines.shape[1], -1)

time: 19 us -> 19 us (level)
  no operation moved by 1% of the time
where the time goes in v9:
time: 19 us; the launch traced here: 18.8 us
  Pallas kernels  18.2 us (96%)
  between operations  0.64 us (3%)
    pallas_call x1, Pallas kernels, per_device(): pl.pallas_call(functools.partial(kernel, sizes), out_shape=(pltpu.VMEM(sp...  16.7 us
    pallas_call x1, Pallas kernels, per_device(): pl.pallas_call(functools.partial(finish, (ranks, halves, slots, rounds, p...  1.51 us

profile of v9, /device:TPU:0, one launch (start us, length us, event | category | flops | bytes accessed | tf_op | source)
XLA Modules:
  0.0 18.8 jit_solution(12018361430083871981)
XLA Ops:
  0.6 16.7 %shard_map.59 = (bf16[5,48,640]{2,1,0:T(8,128)(2,1)S(1)}, bf16[16,16,128]{2,1,0:T(8,128)(2,1)S(1)}, bf16[2,128,512]{2,1,0:T(8,128)(2,1)S(1)}) custom-call(bf16[3,8,2,2,256]{4,3,2,1,0:T(2,128)(2,1)} %grid_hbm.1, bf16[40,1,32,640]{3,2,1,0:T(8,128)(2,1)} %basis_ref.1, s32[640]{0:T(1024)} %owner_hbm.1, f32[8]{0:T(128)} %speed_hbm.1), custom_call_target="tpu_custom_call" | custom-call | tf_op jit(solution)/shard_map/pallas_call | solution.py:403
  17.3 1.5 %shard_map.60 = (bf16[40,48,640]{2,1,0:T(8,128)(2,1)}, bf16[3,8,2,2,256]{4,3,2,1,0:T(2,128)(2,1)}) custom-call(bf16[16,16,128]{2,1,0:T(8,128)(2,1)S(1)} %get-tuple-element.7.arrived_ref, bf16[2,128,512]{2,1,0:T(8,128)(2,1)S(1)} %get-tuple-element.8.table, bf16[5,48,640]{2,1,0:T(8,128)(2,1)S(1)} %get-tuple-element.9.spectra_ref), custom_call_target="tpu_custom_call" | custom-call | tf_op jit(solution)/shard_map/pallas_call | solution.py:439
